TPU v7x, 512 devices: a whole 4x8x8 slice. The times are simulated.
512 devices in a mesh: dp: 32 (over y, z_lo, core), group: 16 (over z_hi, x).
Axes of the slice: x: 4, y: 8, z: 8 (z_hi: 4, z_lo: 2; z = z_hi * 2 + z_lo), core: 2. Of those that a mesh axis runs over, the one named last changes fastest.
Arguments:
- glu_in: bfloat16 [131072, 3072], P(('dp', 'group'))
- cotangent: bfloat16 [131072, 1536], P(('dp', 'group')), may hold values from -6 to 6
- frame_count: int32 [1024], P(('dp', 'group')), may hold values from 64 to 128, as said below
- kernel: bfloat16 [16, 32, 1536], P('group'), may hold values from -1 to 1
- norm_params: bfloat16 [16, 2, 1536], P('group'), may hold values from 0.5 to 1.5
- drift_kernel: bfloat16 [16, 32, 1536], P('group'), may hold values from -8 to 8
- drift_norm: bfloat16 [16, 2, 1536], P('group'), may hold values from -8 to 8
Outputs:
- kernel_average: float32 [32, 1536], P(None, 'dp')
- norm_average: float32 [2, 1536], P(None, 'dp')
Inputs may be any that keep to these rules, and one draw needn't show every extreme that they name: `frame_count`: frame counts of the utterance slots; some utterance fills all 128 frames.
All inputs are finite; a program needn't handle non-finite values.
Results may differ from a plain program's by a relative error of at most 0.007.
Values sent between devices are 32-bit elements; how exact they have to be, the bound alone decides.
No kernel may reach another device: no remote copies, remote signals or barrier semaphores. Data moves between devices by JAX's collectives and lax.ppermute only.
A program may use at most 64 MiB of HBM per device.

v0:
```python
import jax
import jax.numpy as jnp
from jax import lax
from jax.sharding import PartitionSpec as P

K = 32


grad_factor_base = 128.0
eps_norm = 1e-05


def gated_input(inputs, counts):
    utterances = counts.shape[0]
    channels = inputs.shape[1] // 2
    slot_len = inputs.shape[0] // utterances
    position = lax.broadcasted_iota(jnp.int32, (utterances, slot_len), 1)
    live_mask = (position < counts[:, None]).astype(jnp.float32)[:, :, None]
    values = inputs[:, :channels].astype(jnp.float32).reshape(utterances, slot_len, channels)
    gate_part = inputs[:, channels:].astype(jnp.float32).reshape(utterances, slot_len, channels)
    return (values * jax.nn.sigmoid(gate_part) * live_mask, live_mask)


def pad_field(gated_field):
    left_pad = K // 2
    return jnp.pad(gated_field, ((0, 0), (left_pad, K - 1 - left_pad), (0, 0)))


def depthwise(padded, kernel_f, slot_len):
    summed = padded[:, 0:slot_len, :] * kernel_f[0]
    for tap_index in range(1, K):
        summed = summed + padded[:, tap_index : tap_index + slot_len, :] * kernel_f[tap_index]
    return summed


def kernel_terms(padded, conv_back, slot_len):
    return jnp.stack(
        [
            jnp.sum(padded[:, tap_index : tap_index + slot_len, :] * conv_back, axis=(0, 1))
            for tap_index in range(K)
        ]
    )


def across_groups(kernel_part, norm_part, frames):
    kernel_summed, norm_summed, weight_total = lax.psum((kernel_part, norm_part, frames), "group")
    return (kernel_summed / weight_total, norm_summed / weight_total)


def on_device(glu_in, cotangent, frame_count, kernel, norm_params, drift_kernel, drift_norm):
    utterances = frame_count.shape[0]
    slot_len = glu_in.shape[0] // utterances
    channels = cotangent.shape[1]
    gated_field, live_mask = gated_input(glu_in, frame_count)
    padded = pad_field(gated_field)
    conv_out = depthwise(padded, kernel[0].astype(jnp.float32), slot_len)
    local_frames = jnp.sum(frame_count).astype(jnp.float32)
    local_first = jnp.sum(conv_out * live_mask, axis=(0, 1))
    frames, first_sum = lax.psum((local_frames, local_first), "dp")
    mean_value = first_sum / frames
    centered = (conv_out - mean_value) * live_mask
    second_sum = lax.psum(jnp.sum(centered * centered, axis=(0, 1)), "dp")
    variance = second_sum / frames
    inverse = lax.rsqrt(variance + eps_norm)
    normed = (conv_out - mean_value) * inverse
    params_f = norm_params[0].astype(jnp.float32)
    norm_gain = params_f[0]
    norm_shift = params_f[1]
    norm_out = norm_gain * normed + norm_shift
    sigmoid_out = jax.nn.sigmoid(norm_out)
    swish_slope = sigmoid_out * (1.0 + norm_out * (1.0 - sigmoid_out))
    cot_rows = cotangent.astype(jnp.float32).reshape(utterances, slot_len, channels)
    upstream = cot_rows * live_mask * swish_slope
    local_norm = jnp.stack(
        [jnp.sum(upstream * normed, axis=(0, 1)), jnp.sum(upstream, axis=(0, 1))]
    )
    share_len = channels // lax.axis_size("dp")
    share_start = lax.axis_index("dp") * share_len
    norm_sums = lax.psum(local_norm, "dp")
    conv_back = (
        norm_gain
        * inverse
        * (upstream - (norm_sums[1] + normed * norm_sums[0]) / frames)
        * live_mask
    )
    local_kernel = kernel_terms(padded, conv_back, slot_len)
    kernel_sum = lax.psum(local_kernel, "dp")
    grad_factor = grad_factor_base / frames
    kernel_delta = (drift_kernel[0].astype(jnp.float32) + kernel_sum * grad_factor).astype(
        jnp.bfloat16
    )
    norm_delta = (drift_norm[0].astype(jnp.float32) + norm_sums * grad_factor).astype(jnp.bfloat16)
    kernel_average, norm_average = across_groups(
        kernel_delta.astype(jnp.float32) * frames, norm_delta.astype(jnp.float32) * frames, frames
    )
    kernel_out = lax.dynamic_slice_in_dim(kernel_average, share_start, share_len, 1)
    norm_final = lax.dynamic_slice_in_dim(norm_average, share_start, share_len, 1)
    return (kernel_out, norm_final)


def solution(mesh):
    placed = (
        P(("dp", "group"), None),
        P(("dp", "group"), None),
        P(("dp", "group")),
        P("group", None, None),
        P("group", None, None),
        P("group", None, None),
        P("group", None, None),
    )
    return jax.shard_map(
        on_device,
        mesh=mesh,
        in_specs=placed,
        out_specs=(P(None, "dp"), P(None, "dp")),
        check_vma=False,
    )
```

profile of v0, /device:TPU:24, one launch (start us, length us, event | category | flops | bytes accessed | tf_op | source)
XLA Modules:
  0.0 651.9 jit_solution(11269609396778895678)
XLA Ops:
  7.2 0.0 all-reduce.6.cloned.1.call-start
  7.2 0.9 convert_element_type.54
  8.1 0.2 slice_reduce_fusion.33
  8.3 0.3 slice_reduce_fusion.34
  8.7 0.7 compare_convert_fusion
  9.4 1.3 reduce_sum.334
  11.3 0.7 convert_element_type.53
  12.1 1.8 convert_multiply_fusion.1
  13.9 0.2 broadcast_multiply_fusion
  14.0 6.4 multiply_reduce_fusion.34
  20.4 51.3 %all-reduce.1 = (f32[]{:T(128)}, f32[1536]{0:T(1024)S(1)}) all-reduce(f32[]{:T(128)S(6)} %convert_element_type.55, f32[1536]{0:T(1024)S(1)} %get-tuple-element.79), channel_id=1, replica_groups=mesh['dp'=32,'group'=16] {'dp'}, use_global_device_ids=true, to_apply=%region_3.4 | all-reduce | flops 1537 | bytes 12296 | tf_op jit(solution)/shard_map/psum | solution.py:59
  71.7 0.6 broadcast_divide_fusion
  72.4 0.3 multiply_reduce_fusion.33
  72.7 54.8 %psum.58 = f32[1536]{0:T(1024)S(1)} all-reduce(f32[1536]{0:T(1024)S(1)} %multiply_reduce_fusion.33), channel_id=1, replica_groups=mesh['dp'=32,'group'=16] {'dp'}, use_global_device_ids=true, to_apply=%region_5.6 | all-reduce | flops 1536 | bytes 12288 | tf_op jit(solution)/shard_map/psum | solution.py:62
  127.5 0.7 fusion.4
  128.1 2.1 multiply_reduce_fusion.32
  130.3 103.8 %psum.59 = f32[2,1536]{1,0:T(2,128)S(1)} all-reduce(f32[2,1536]{1,0:T(2,128)S(1)} %pad_maximum_fusion), channel_id=1, replica_groups=mesh['dp'=32,'group'=16] {'dp'}, use_global_device_ids=true, to_apply=%region_8.9 | all-reduce | flops 3072 | bytes 24576 | tf_op jit(solution)/shard_map/psum | solution.py:79
  234.2 6.9 %multiply_reduce_fusion = (f32[1536]{0:T(1024)S(1)}, f32[1536]{0:T(1024)S(1)}, f32[1536]{0:T(1024)S(1)}, f32[1536]{0:T(1024)S(1)}, f32[1536]{0:T(1024)S(1)}, /*i...) fusion(f32[2,128,1536]{2,1,0:T(8,128)S(1)} %broadcast_multiply_, ...), kind=kLoop, calls=%fused_computation.34 | loop fusion | flops 21992448 | bytes 5659652 | tf_op jit(solution)/shard_map/reduce_sum | solution.py:39
  241.1 0.0 copy-start
  241.1 2.8 multiply_reduce_fusion.18
  243.9 0.0 copy-start.1
  244.3 2.7 stack.143
  247.1 0.0 all-reduce.6.cloned.1.call-update
  247.1 0.0 all-reduce.8.cloned.1.call-start
  247.8 223.7 %all-reduce.6.cloned.1.call-done = f32[32,1536]{1,0:T(8,128)} async-done(((f32[32,1536]{1,0:T(8,128)}), f32[32,1536]{1,0:T(8,128)}) %all-reduce.6.cloned.1.call-update) | async-done | bytes 196624 | tf_op jit(solution)/shard_map/psum | solution.py:87
  471.5 0.0 copy-done
  471.5 2.3 convert_multiply_fusion.2
  473.8 0.0 all-reduce.8.cloned.1.call-update
  473.8 0.0 copy-done.1
  473.8 0.7 convert_multiply_fusion.3
  474.5 83.4 %all-reduce.2 = (f32[]{:T(128)}, f32[2,1536]{1,0:T(2,128)S(1)}) all-reduce(f32[]{:T(128)} %get-tuple-element.72, f32[2,1536]{1,0:T(2,128)S(1)} %convert_multiply_fusion.3), channel_id=1, replica_groups=mesh['dp'=32,'group'=16] {'group'}, use_global_device_ids=true, to_apply=%region_43.44 | all-reduce | flops 3073 | bytes 24584 | tf_op jit(solution)/shard_map/psum | solution.py:46
  557.9 1.3 dynamic-slice_divide_fusion.1
  559.2 83.8 %all-reduce.8.cloned.1.call-done = f32[32,1536]{1,0:T(8,128)} async-done(((f32[32,1536]{1,0:T(8,128)}), f32[32,1536]{1,0:T(8,128)}) %all-reduce.8.cloned.1.call-update) | async-done | bytes 196624 | tf_op jit(solution)/shard_map/psum | solution.py:46
  643.0 2.1 dynamic-slice_divide_fusion
  (37 shorter events, 0.3 us)
Async XLA Ops:
  7.2 464.4 %all-reduce.6.cloned.1.call-start = ((), (), s32[]{:S(2)}) async-start(), calls=%async_computation | async-start | bytes 393216 | tf_op jit(solution)/shard_map/psum | solution.py:87
  241.1 230.5 %copy-start = (bf16[1,32,1536]{2,1,0:T(8,128)(2,1)S(1)}, bf16[1,32,1536]{2,1,0:T(8,128)(2,1)}, u32[]{:S(2)}) copy-start(bf16[1,32,1536]{2,1,0:T(8,128)(2,1)} %param.12) | copy-start | bytes 294916
  243.9 230.0 %copy-start.1 = (bf16[1,2,1536]{2,1,0:T(2,128)(2,1)S(1)}, bf16[1,2,1536]{2,1,0:T(2,128)(2,1)}, u32[]{:S(2)}) copy-start(bf16[1,2,1536]{2,1,0:T(2,128)(2,1)} %param.13) | copy-start | bytes 18436
  247.1 395.9 %all-reduce.8.cloned.1.call-start = ((), (), s32[]{:S(2)}) async-start(), calls=%async_computation.1 | async-start | bytes 393216 | tf_op jit(solution)/shard_map/psum | solution.py:46
Sparse Core Ops, SparseCore 0:
  247.2 224.2 all-reduce.5
  474.7 168.2 all-reduce.7
where the time goes:
time: 653 us; the launch traced here: 652 us
  waiting for transfers between devices  308 us (47%)
  blocking collectives  293 us (45%)
  other arithmetic  31.6 us (5%)
  between operations  15.8 us (2%)
    psum x1, waiting for transfers between devices, on_device(): kernel_sum = lax.psum(local_kernel, 'dp')  224 us
    psum x1, blocking collectives, on_device(): norm_sums = lax.psum(local_norm, 'dp')  104 us
    psum x1, waiting for transfers between devices, across_groups(): lax.psum((kernel_part, norm_part, frames), 'group')  83.8 us
    psum x1, blocking collectives, across_groups(): lax.psum((kernel_part, norm_part, frames), 'group')  83.4 us
    psum x1, blocking collectives, on_device(): second_sum = lax.psum(jnp.sum(centered * centered, axis=(0, 1)), 'dp')  54.8 us
    psum x1, blocking collectives, on_device(): frames, first_sum = lax.psum((local_frames, local_first), 'dp')  51.3 us
  transfers between devices with their start and end apart: 2, of which 2 were waited for; matrix products, arithmetic and copies ran while one was open for 0% of the time, Pallas kernels for 0%

commit v1 on v0

v1 whole, which is shorter than its diff:
```python
import functools

import jax
import jax.numpy as jnp
from jax import lax
from jax.experimental import pallas as pl
from jax.experimental.pallas import tpu as pltpu
from jax.sharding import PartitionSpec as P

K = 32
HALF = K // 2
SUB = 8
LANES = 128
SLOT = 128
UTT = 2
ROWS = UTT * SLOT
PADDED = HALF + SLOT + HALF
WIDE = SLOT + SUB
STAT_ROWS = 32

grad_factor_base = 128.0
eps_norm = 1e-05


def lane_tile(i):
    return pl.ds(pl.multiple_of(i * LANES, LANES), LANES)


def live_rows(count):
    return lax.broadcasted_iota(jnp.int32, (SLOT, LANES), 0) < count


def conv_kernel(count_ref, glu_ref, kernel_ref, padded_ref, conv_ref, stat_ref, taps_ref):
    channels = conv_ref.shape[1]
    taps_ref[...] = kernel_ref[0].astype(jnp.float32)
    counts = [count_ref[u] for u in range(UTT)]
    local_frames = sum(counts).astype(jnp.float32)
    stat_ref[...] = jnp.full(stat_ref.shape, local_frames, jnp.float32)

    def tile(i, carry):
        lanes = lane_tile(i)
        gate_lanes = lane_tile(i + channels // LANES)
        total = jnp.zeros((SUB, LANES), jnp.float32)
        fields = []
        for u in range(UTT):
            live = live_rows(counts[u])
            rows = pl.ds(u * SLOT, SLOT)
            value = glu_ref[rows, lanes].astype(jnp.float32)
            gate = glu_ref[rows, gate_lanes].astype(jnp.float32)
            base = u * PADDED
            edge = jnp.zeros((HALF, LANES), jnp.float32)
            padded_ref[pl.ds(base, HALF), lanes] = edge
            padded_ref[pl.ds(base + HALF + SLOT, HALF), lanes] = edge
            padded_ref[pl.ds(base + HALF, SLOT), lanes] = jnp.where(
                live, value * jax.nn.sigmoid(gate), 0.0
            )
            summed = None
            for r in range(SUB):
                part = None
                for j in range(K // SUB):
                    tap = taps_ref[pl.ds(r + SUB * j, 1), lanes]
                    term = padded_ref[pl.ds(base + SUB * j, WIDE), lanes] * tap
                    part = term if part is None else part + term
                if r:
                    part = pltpu.roll(part, WIDE - r, 0)
                part = part[:SLOT]
                summed = part if summed is None else summed + part
            conv_ref[rows, lanes] = summed
            masked = jnp.where(live, summed, 0.0)
            total = total + jnp.sum(masked.reshape(SLOT // SUB, SUB, LANES), axis=0)
            fields.append((live, summed))
        local_mean = jnp.sum(total, axis=0, keepdims=True) / local_frames
        spread = jnp.zeros((SUB, LANES), jnp.float32)
        for live, summed in fields:
            centered = jnp.where(live, summed - local_mean, 0.0)
            spread = spread + jnp.sum((centered * centered).reshape(SLOT // SUB, SUB, LANES), axis=0)
        stat_ref[pl.ds(i, 1), :] = local_mean
        stat_ref[pl.ds(i + channels // LANES, 1), :] = jnp.sum(spread, axis=0, keepdims=True)
        return carry

    lax.fori_loop(0, channels // LANES, tile, 0)


def merge_stats(parts, tiles):
    frames = sum(part[2 * tiles : 2 * tiles + 1] for part in parts)
    mean = sum(part[:tiles] * part[2 * tiles : 2 * tiles + 1] for part in parts) / frames
    spread = sum(
        part[tiles : 2 * tiles]
        + part[2 * tiles : 2 * tiles + 1] * (part[:tiles] - mean) * (part[:tiles] - mean)
        for part in parts
    )
    return frames, mean, spread


def pair_kernel(tiles, own_ref, other_ref, out_ref):
    frames, mean, spread = merge_stats([own_ref[...], other_ref[...]], tiles)
    rest = jnp.broadcast_to(frames, (STAT_ROWS - 2 * tiles, LANES))
    for peer in range(out_ref.shape[0]):
        out_ref[peer, pl.ds(0, tiles), :] = mean
        out_ref[peer, pl.ds(tiles, tiles), :] = spread
        out_ref[peer, pl.ds(2 * tiles, STAT_ROWS - 2 * tiles), :] = rest


def back_kernel(
    count_ref, stat_ref, cot_ref, param_ref, padded_ref, conv_ref, out_ref, mean_ref, inv_ref, par_ref, turn_ref
):
    channels = conv_ref.shape[1]
    tiles = channels // LANES
    counts = [count_ref[u] for u in range(UTT)]
    local_frames = sum(counts).astype(jnp.float32)
    frames, mean, spread = merge_stats([stat_ref[p] for p in range(stat_ref.shape[0])], tiles)
    mean_ref[pl.ds(0, tiles), :] = mean
    inv_ref[pl.ds(0, tiles), :] = lax.rsqrt(spread / frames + eps_norm)
    par_ref[...] = param_ref[0].astype(jnp.float32)
    position = lax.broadcasted_iota(jnp.int32, (K, SLOT), 1) + HALF
    position = position - lax.broadcasted_iota(jnp.int32, (K, SLOT), 0)

    def tile(i, carry):
        lanes = lane_tile(i)
        mean_row = mean_ref[pl.ds(i, 1), :]
        inv_row = inv_ref[pl.ds(i, 1), :]
        gain_row = par_ref[pl.ds(0, 1), lanes]
        shift_row = par_ref[pl.ds(1, 1), lanes]
        gain_sum = jnp.zeros((SUB, LANES), jnp.float32)
        shift_sum = jnp.zeros((SUB, LANES), jnp.float32)
        live_sum = jnp.zeros((K, LANES), jnp.float32)
        up_taps = [jnp.zeros((SUB, LANES), jnp.float32) for _ in range(K)]
        norm_taps = [jnp.zeros((SUB, LANES), jnp.float32) for _ in range(K)]
        for u in range(UTT):
            live = live_rows(counts[u])
            rows = pl.ds(u * SLOT, SLOT)
            base = u * PADDED
            normed = (conv_ref[rows, lanes] - mean_row) * inv_row
            norm_out = gain_row * normed + shift_row
            sig = jax.nn.sigmoid(norm_out)
            slope = sig * (1.0 + norm_out * (1.0 - sig))
            upstream = jnp.where(live, cot_ref[rows, lanes].astype(jnp.float32) * slope, 0.0)
            normed = jnp.where(live, normed, 0.0)
            gain_sum = gain_sum + jnp.sum(
                (upstream * normed).reshape(SLOT // SUB, SUB, LANES), axis=0
            )
            shift_sum = shift_sum + jnp.sum(upstream.reshape(SLOT // SUB, SUB, LANES), axis=0)
            edge = jnp.zeros((SUB, LANES), jnp.float32)
            up_wide = jnp.concatenate([upstream, edge], axis=0)
            norm_wide = jnp.concatenate([normed, edge], axis=0)
            for r in range(SUB):
                up_r = pltpu.roll(up_wide, r, 0) if r else up_wide
                norm_r = pltpu.roll(norm_wide, r, 0) if r else norm_wide
                for j in range(K // SUB):
                    k = r + SUB * j
                    field = padded_ref[pl.ds(base + SUB * j, WIDE), lanes]
                    up_taps[k] = up_taps[k] + jnp.sum(
                        (up_r * field).reshape(WIDE // SUB, SUB, LANES), axis=0
                    )
                    norm_taps[k] = norm_taps[k] + jnp.sum(
                        (norm_r * field).reshape(WIDE // SUB, SUB, LANES), axis=0
                    )
            inside = jnp.where((position >= 0) & (position < counts[u]), 1.0, 0.0)
            live_sum = live_sum + jnp.dot(
                inside,
                padded_ref[pl.ds(base + HALF, SLOT), lanes],
                preferred_element_type=jnp.float32,
                precision=lax.Precision.HIGHEST,
            )
        scale = gain_row * inv_row
        up_all = jnp.concatenate([jnp.sum(x, axis=0, keepdims=True) for x in up_taps], axis=0)
        norm_all = jnp.concatenate([jnp.sum(x, axis=0, keepdims=True) for x in norm_taps], axis=0)
        row = lax.broadcasted_iota(jnp.int32, (K, LANES), 0)
        extra = jnp.where(row == 0, jnp.sum(gain_sum, axis=0, keepdims=True), local_frames)
        extra = jnp.where(row == 1, jnp.sum(shift_sum, axis=0, keepdims=True), extra)
        block = jnp.concatenate([up_all * scale, live_sum * scale, norm_all * scale, extra], axis=0)
        turn_ref[lane_tile(i), :] = block.T
        return carry

    lax.fori_loop(0, tiles, tile, 0)
    core = lax.rem(lax.axis_index("dp"), 2)
    chunks = 2 * out_ref.shape[1]
    share = channels // chunks
    for j in range(chunks):
        side = core if j % 2 == 0 else 1 - core
        out_ref[side, j // 2] = turn_ref[pl.ds(j * share, share), :]


def delta_kernel(sum_ref, drift_ref, drift_norm_ref, out_ref):
    share = sum_ref.shape[1]
    channels = drift_ref.shape[2]
    total = sum(sum_ref[p] for p in range(sum_ref.shape[0]))
    frames = total[:, 3 * K + 2 : 3 * K + 3]
    gain_sum = total[:, 3 * K : 3 * K + 1]
    shift_sum = total[:, 3 * K + 1 : 3 * K + 2]
    live_part = pltpu.roll(total, LANES - K, 1)
    norm_part = pltpu.roll(total, LANES - 2 * K, 1)
    kernel_sum = total - (shift_sum * live_part + gain_sum * norm_part) / frames
    start = lax.axis_index("dp") * share
    first = jnp.minimum(start // LANES, channels // LANES - 2)
    window = pl.ds(pl.multiple_of(first * LANES, LANES), 2 * LANES)
    drift = jnp.concatenate(
        [
            drift_ref[0, :, window].astype(jnp.float32),
            drift_norm_ref[0, :, window].astype(jnp.float32),
            jnp.zeros((LANES - K - 2, 2 * LANES), jnp.float32),
        ],
        axis=0,
    )
    drift = pltpu.roll(drift, lax.rem(2 * LANES - (start - first * LANES), 2 * LANES), 1)
    drift = drift[:, :LANES].T[:share]
    lane = lax.broadcasted_iota(jnp.int32, (share, LANES), 1)
    norm_at = pltpu.roll(total, LANES - 2 * K, 1)
    sums = jnp.where(lane < K, kernel_sum, norm_at)
    delta = (drift + (grad_factor_base / frames) * sums).astype(jnp.bfloat16).astype(jnp.float32)
    weighted = delta * frames
    block = share // 3
    lane = lane[:block]
    packed = jnp.broadcast_to(frames[:block], (block, LANES))
    for b in range(3):
        piece = weighted[b * block : (b + 1) * block]
        moved = pltpu.roll(piece, b * K, 1) if b else piece
        packed = jnp.where((lane >= b * K) & (lane < (b + 1) * K), moved, packed)
        at = 3 * K + 2 * b
        moved = pltpu.roll(piece, at - K, 1)
        packed = jnp.where((lane >= at) & (lane < at + 2), moved, packed)
    for peer in range(out_ref.shape[0]):
        out_ref[peer] = packed


def average_kernel(sum_ref, kernel_ref, norm_ref):
    total = sum(sum_ref[p] for p in range(sum_ref.shape[0]))
    block = total.shape[0]
    average = total / total[:, 3 * K + 6 : 3 * K + 7]
    average = jnp.concatenate([average, jnp.zeros((LANES - block, LANES), jnp.float32)], axis=0)
    turned = average.T
    for b in range(3):
        kernel_ref[:, b * block : (b + 1) * block] = turned[b * K : (b + 1) * K, :block]
        norm_ref[:, b * block : (b + 1) * block] = turned[3 * K + 2 * b : 3 * K + 2 * b + 2, :block]


def on_device(glu_in, cotangent, frame_count, kernel, norm_params, drift_kernel, drift_norm):
    channels = cotangent.shape[1]
    tiles = channels // LANES
    n_dp = lax.axis_size("dp")
    n_group = lax.axis_size("group")
    peers = n_dp // 2
    share = channels // n_dp
    same_core = [[2 * p + core for p in range(peers)] for core in range(2)]
    swap = [(i, i ^ 1) for i in range(n_dp)]
    vmem = pl.BlockSpec(memory_space=pltpu.VMEM)
    smem = pl.BlockSpec(memory_space=pltpu.SMEM)
    params = pltpu.CompilerParams(vmem_limit_bytes=48 * 1024 * 1024)
    f32 = jnp.float32

    padded, conv_out, stats = pl.pallas_call(
        conv_kernel,
        out_shape=(
            jax.ShapeDtypeStruct((UTT * PADDED, channels), f32),
            jax.ShapeDtypeStruct((ROWS, channels), f32),
            jax.ShapeDtypeStruct((STAT_ROWS, LANES), f32),
        ),
        in_specs=[smem, vmem, vmem],
        out_specs=(vmem, vmem, vmem),
        scratch_shapes=[pltpu.VMEM((K, channels), f32)],
        compiler_params=params,
        name="conv_stats",
    )(frame_count, glu_in, kernel)

    other = lax.ppermute(stats, "dp", swap)
    spread_out = pl.pallas_call(
        functools.partial(pair_kernel, tiles),
        out_shape=jax.ShapeDtypeStruct((peers, STAT_ROWS, LANES), f32),
        in_specs=[vmem, vmem],
        out_specs=vmem,
        compiler_params=params,
        name="pair_stats",
    )(stats, other)
    gathered = lax.all_to_all(spread_out, "dp", 0, 0, axis_index_groups=same_core)

    both = pl.pallas_call(
        back_kernel,
        out_shape=jax.ShapeDtypeStruct((2, peers, share, LANES), f32),
        in_specs=[smem, vmem, vmem, vmem, vmem, vmem],
        out_specs=vmem,
        scratch_shapes=[
            pltpu.VMEM((16, LANES), f32),
            pltpu.VMEM((16, LANES), f32),
            pltpu.VMEM((2, channels), f32),
            pltpu.VMEM((channels, LANES), f32),
        ],
        compiler_params=params,
        name="tap_sums",
    )(frame_count, gathered, cotangent, norm_params, padded, conv_out)
    arrived = lax.ppermute(both[1], "dp", swap)
    tap_sums = lax.all_to_all(both[0] + arrived, "dp", 0, 0, axis_index_groups=same_core)

    weighted = pl.pallas_call(
        delta_kernel,
        out_shape=jax.ShapeDtypeStruct((n_group, share // 3, LANES), f32),
        in_specs=[vmem, vmem, vmem],
        out_specs=vmem,
        compiler_params=params,
        name="group_delta",
    )(tap_sums, drift_kernel, drift_norm)
    weighted = lax.all_to_all(weighted, "group", 0, 0)

    return pl.pallas_call(
        average_kernel,
        out_shape=(
            jax.ShapeDtypeStruct((K, share), f32),
            jax.ShapeDtypeStruct((2, share), f32),
        ),
        in_specs=[vmem],
        out_specs=(vmem, vmem),
        compiler_params=params,
        name="group_average",
    )(weighted)


def solution(mesh):
    placed = (
        P(("dp", "group"), None),
        P(("dp", "group"), None),
        P(("dp", "group")),
        P("group", None, None),
        P("group", None, None),
        P("group", None, None),
        P("group", None, None),
    )
    return jax.shard_map(
        on_device,
        mesh=mesh,
        in_specs=placed,
        out_specs=(P(None, "dp"), P(None, "dp")),
        check_vma=False,
    )
```

time: 653 us -> 92.7 us (0.14)
  the two profiles are of different devices: /device:TPU:24 before, /device:TPU:2 now
where the time goes in v1:
time: 92.7 us; the launch traced here: 92.3 us
  blocking collectives  60.6 us (65%)
  Pallas kernels  21.3 us (23%)
  starting transfers between devices  3.84 us (4%)
  local copies, waits for them, and re-layouts  3 us (3%)
  waiting for transfers between devices  2.84 us (3%)
    all_to_all x1, blocking collectives, on_device(): lax.all_to_all(spread_out, 'dp', 0, 0, axis_index_groups=same_core)  21.1 us
    all_to_all x1, blocking collectives, on_device(): weighted = lax.all_to_all(weighted, 'group', 0, 0)  21.1 us
    all_to_all x1, blocking collectives, on_device(): lax.all_to_all(both[0] + arrived, 'dp', 0, 0, axis_index_groups=same_core)  18.4 us
    pallas_call x1, Pallas kernels, on_device(): pl.pallas_call(back_kernel, out_shape=jax.ShapeDtypeStruct((2, peers, sha...  13.8 us
    pallas_call x1, Pallas kernels, on_device(): pl.pallas_call(conv_kernel, out_shape=(jax.ShapeDtypeStruct((UTT * PADDED...  6.31 us
    unnamed x16, local copies, waits for them, and re-layouts  2.97 us
    ppermute x1, starting transfers between devices, on_device(): arrived = lax.ppermute(both[1], 'dp', swap)  1.92 us
    ppermute x1, starting transfers between devices, on_device(): other = lax.ppermute(stats, 'dp', swap)  1.92 us
  transfers between devices with their start and end apart: 2, of which 2 were waited for; matrix products, arithmetic and copies ran while one was open for 0% of the time, Pallas kernels for 0%

profile of v1, /device:TPU:2, one launch (start us, length us, event | category | flops | bytes accessed | tf_op | source)
XLA Modules:
  0.0 92.3 jit_solution(7306521068397382076)
XLA Ops:
  0.6 0.0 copy-start
  0.6 1.4 %copy-done = bf16[256,3072]{1,0:T(8,128)(2,1)S(1)} copy-done((bf16[256,3072]{1,0:T(8,128)(2,1)S(1)}, bf16[256,3072]{1,0:T(8,128)(2,1)}, u32[]{:S(2)}) %copy-start) | copy-done | bytes 1572888
  2.0 0.0 copy-start.2
  2.0 0.9 copy-done.2
  2.9 0.0 copy-start.6
  2.9 0.7 copy-done.6
  3.6 0.0 copy-start.1
  3.6 0.0 copy-start.4
  3.6 0.0 copy-start.7
  3.6 6.3 %conv_stats.1 = (f32[320,1536]{1,0:T(8,128)S(1)}, f32[256,1536]{1,0:T(8,128)S(1)}, f32[32,128]{1,0:T(8,128)S(1)}) custom-call(s32[2]{0:T(128)S(1)} %copy-done.6, bf16[256,3072]{1,0:T(8,128)(2,1)S(1)} %copy-done, bf16[1,32,1536]{2,1,0:T(8,128)(2,1)S(1)} %copy-done.2), custom_call_target="tpu_custom_call" | custom-call | tf_op jit(solution)/shard_map/conv_stats/pallas_call | solution.py:251
  9.9 1.9 %collective-permute-start = (f32[32,128]{1,0:T(8,128)S(1)}, f32[32,128]{1,0:T(8,128)S(1)}, u32[]{:S(2)}, u32[]{:S(2)}) collective-permute-start(f32[32,128]{1,0:T(8,128)S(1)} %get-tuple-element.5.own_ref), channel_id=1, source_target_pairs={{0,16},{16,0},{32,48},{48,32},{64,80},{80,64},{96,112},{112,96},{1... | collective-permute-start | bytes 49160 | tf_op jit(solution)/shard_map/ppermute | solution.py:265
  11.8 1.1 %collective-permute-done.other_ref = f32[32,128]{1,0:T(8,128)S(1)} collective-permute-done((f32[32,128]{1,0:T(8,128)S(1)}, f32[32,128]{1,0:T(8,128)S(1)}, u32[]{:S(2)}, u32[]{:S(2)}) %collective-permute-start) | collective-permute-done | bytes 16416 | tf_op jit(solution)/shard_map/ppermute | solution.py:265
  13.0 21.1 %all_to_all.15.stat_ref = f32[16,32,128]{2,1,0:T(8,128)S(1)} all-to-all(f32[16,32,128]{2,1,0:T(8,128)S(1)} %pair_stats.1), channel_id=1, replica_groups={{0,32,64,96,128,160,192,224,256,288,320,352,384,416,448,480},{16,48,80,..., dimensions={0} | all-to-all | bytes 524288 | tf_op jit(solution)/shard_map/all_to_all | solution.py:274
  34.1 0.0 copy-done.1
  34.1 0.0 copy-done.4
  34.2 0.0 copy-done.7
  34.2 13.8 %tap_sums.1 = f32[2,16,48,128]{3,2,1,0:T(8,128)S(1)} custom-call(s32[2]{0:T(128)S(1)} %copy-done.7, f32[16,32,128]{2,1,0:T(8,128)S(1)} %all_to_all.15.stat_ref, bf16[256,1536]{1,0:T(8,128)(2,1)S(1)} %copy-done.1, bf16[1,2,1536]{2,1,0:T(2,128)(2,1)S(1)} %copy-done.4, f32[320,1536]{1,0:T(8,128)S(1)} %get-tuple-element.6.padded_ref, ...), custom_call_target="tpu_custom_call" | custom-call | tf_op jit(solution)/shard_map/tap_sums/pallas_call | solution.py:276
  48.0 0.0 copy-start.3
  48.0 0.0 copy-start.5
  48.0 1.9 %collective-permute-start.1 = (f32[16,48,128]{2,1,0:T(8,128)S(1)}, f32[16,48,128]{2,1,0:T(8,128)S(1)}, u32[]{:S(2)}, u32[]{:S(2)}) collective-permute-start(f32[16,48,128]{2,1,0:T(8,128)S(1)} %slice_bitcast_fusion), channel_id=1, source_target_pairs={{0,16},{16,0},{32,48},{48,32},{64,80},{80,64},{96,112},{112,96},{1... | collective-permute-start | bytes 1179656 | tf_op jit(solution)/shard_map/ppermute | solution.py:290
  49.9 1.7 %collective-permute-done.1 = f32[16,48,128]{2,1,0:T(8,128)S(1)} collective-permute-done((f32[16,48,128]{2,1,0:T(8,128)S(1)}, f32[16,48,128]{2,1,0:T(8,128)S(1)}, u32[]{:S(2)}, u32[]{:S(2)}) %collective-permute-start.1) | collective-permute-done | bytes 393248 | tf_op jit(solution)/shard_map/ppermute | solution.py:290
  51.6 0.1 fusion
  51.7 18.4 %all_to_all.16.sum_ref = f32[16,48,128]{2,1,0:T(8,128)S(1)} all-to-all(f32[16,48,128]{2,1,0:T(8,128)S(1)} %fusion), channel_id=1, replica_groups={{0,32,64,96,128,160,192,224,256,288,320,352,384,416,448,480},{16,48,80,..., dimensions={0} | all-to-all | bytes 786432 | tf_op jit(solution)/shard_map/all_to_all | solution.py:291
  70.1 0.0 copy-done.3
  70.1 0.0 copy-done.5
  70.1 0.3 group_delta.1
  70.4 21.1 %all_to_all.17.sum_ref = f32[16,16,128]{2,1,0:T(8,128)S(1)} all-to-all(f32[16,16,128]{2,1,0:T(8,128)S(1)} %group_delta.1), channel_id=1, replica_groups=mesh['dp'=32,'group'=16] {'group'}, dimensions={0} | all-to-all | bytes 262144 | tf_op jit(solution)/shard_map/all_to_all | solution.py:301
  91.5 0.9 group_average.1
  (2 shorter events, 0.1 us)
Async XLA Ops:
  0.6 1.4 %copy-start = (bf16[256,3072]{1,0:T(8,128)(2,1)S(1)}, bf16[256,3072]{1,0:T(8,128)(2,1)}, u32[]{:S(2)}) copy-start(bf16[256,3072]{1,0:T(8,128)(2,1)} %glu_ref.1) | copy-start | bytes 4718596
  2.0 0.9 copy-start.2
  2.9 0.7 copy-start.6
  3.6 30.6 %copy-start.1 = (bf16[256,1536]{1,0:T(8,128)(2,1)S(1)}, bf16[256,1536]{1,0:T(8,128)(2,1)}, u32[]{:S(2)}) copy-start(bf16[256,1536]{1,0:T(8,128)(2,1)} %cot_ref.1) | copy-start | bytes 2359300
  3.6 30.6 %copy-start.4 = (bf16[1,2,1536]{2,1,0:T(2,128)(2,1)S(1)}, bf16[1,2,1536]{2,1,0:T(2,128)(2,1)}, u32[]{:S(2)}) copy-start(bf16[1,2,1536]{2,1,0:T(2,128)(2,1)} %param_ref.1) | copy-start | bytes 18436
  3.6 30.6 %copy-start.7 = (s32[2]{0:T(128)S(1)}, s32[2]{0:T(128)}, u32[]{:S(2)}) copy-start(s32[2]{0:T(128)} %count_ref.3) | copy-start | bytes 28
  9.9 3.1 %collective-permute-start = (f32[32,128]{1,0:T(8,128)S(1)}, f32[32,128]{1,0:T(8,128)S(1)}, u32[]{:S(2)}, u32[]{:S(2)}) collective-permute-start(f32[32,128]{1,0:T(8,128)S(1)} %get-tuple-element.5.own_ref), channel_id=1, source_target_pairs={{0,16},{16,0},{32,48},{48,32},{64,80},{80,64},{96,112},{112,96},{1... | collective-permute-start | bytes 49160 | tf_op jit(solution)/shard_map/ppermute | solution.py:265
  48.0 22.1 %copy-start.3 = (bf16[1,32,1536]{2,1,0:T(8,128)(2,1)S(1)}, bf16[1,32,1536]{2,1,0:T(8,128)(2,1)}, u32[]{:S(2)}) copy-start(bf16[1,32,1536]{2,1,0:T(8,128)(2,1)} %drift_ref.1) | copy-start | bytes 294916
  48.0 22.1 %copy-start.5 = (bf16[1,2,1536]{2,1,0:T(2,128)(2,1)S(1)}, bf16[1,2,1536]{2,1,0:T(2,128)(2,1)}, u32[]{:S(2)}) copy-start(bf16[1,2,1536]{2,1,0:T(2,128)(2,1)} %drift_norm_ref.1) | copy-start | bytes 18436
  48.0 3.6 %collective-permute-start.1 = (f32[16,48,128]{2,1,0:T(8,128)S(1)}, f32[16,48,128]{2,1,0:T(8,128)S(1)}, u32[]{:S(2)}, u32[]{:S(2)}) collective-permute-start(f32[16,48,128]{2,1,0:T(8,128)S(1)} %slice_bitcast_fusion), channel_id=1, source_target_pairs={{0,16},{16,0},{32,48},{48,32},{64,80},{80,64},{96,112},{112,96},{1... | collective-permute-start | bytes 1179656 | tf_op jit(solution)/shard_map/ppermute | solution.py:290

commit v2 on v1

v2 whole, which is shorter than its diff:
```python
import functools
import operator

import jax
import jax.numpy as jnp
from jax import lax
from jax.experimental import pallas as pl
from jax.experimental.pallas import tpu as pltpu
from jax.sharding import PartitionSpec as P

K = 32
HALF = K // 2
SUB = 8
LANES = 128
SLOT = 128
UTT = 2
ROWS = UTT * SLOT
PADDED = HALF + SLOT + HALF
STAT_ROWS = 32
CHUNKS = (4, 8)
R_STEP = 8
UNROLL = 4
TILE_RUN = 3

grad_factor_base = 128.0
eps_norm = 1e-05


def lane_tile(i):
    return pl.ds(pl.multiple_of(i * LANES, LANES), LANES)


def live_rows(count):
    return lax.broadcasted_iota(jnp.int32, (SLOT, LANES), 0) < count


def added(terms):
    return functools.reduce(operator.add, terms)


def fold_rows(field):
    return jnp.sum(field.reshape(field.shape[0] // SUB, SUB, LANES), axis=0)


def scan_rows(field, upward):
    row = lax.broadcasted_iota(jnp.int32, field.shape, 0)
    step = 1
    while step < HALF:
        if upward:
            moved = jnp.where(row < HALF - step, pltpu.roll(field, HALF - step, 0), 0.0)
        else:
            moved = jnp.where(row >= step, pltpu.roll(field, step, 0), 0.0)
        field = field + moved
        step *= 2
    return field


PLAIN, NEXT, SECOND, BOTH = range(4)
PRODUCTS = (
    (PLAIN, 3),
    (SECOND, 1),
    (SECOND, 3),
    (NEXT, 2),
    (BOTH, 0),
    (BOTH, 2),
    (NEXT, 3),
    (BOTH, 1),
    (BOTH, 3),
)
COMBOS = ((0, 1, 2, 3), (0, 1), (2, 3), (0, 2), (0,), (2,), (1, 3), (1,), (3,))


def combine(parts):
    low = parts[0] + parts[1]
    high = parts[0] - parts[2]
    return (
        low + (parts[3] + parts[4]),
        low - (parts[6] + parts[7]),
        high + (parts[3] - parts[5]),
        high - (parts[6] - parts[8]),
    )


def fields_at(field_ref, i, row, product):
    kind, block = product
    return [
        field_ref[i, kind, pl.ds(row + SUB * (4 * m + block), SUB), :] for m in range(SLOT // SUB // 4)
    ]


def conv_kernel(
    count_hbm,
    glu_hbm,
    kernel_hbm,
    cot_hbm,
    field_ref,
    conv_ref,
    stat_ref,
    cot_ref,
    live_sum_ref,
    live_ref,
    count_ref,
    glu_ref,
    kernel_ref,
    taps_ref,
    small_sems,
    glu_sems,
):
    tiles = conv_ref.shape[0]
    channels = tiles * LANES
    count_copy = pltpu.make_async_copy(count_hbm, count_ref, small_sems.at[0])
    kernel_copy = pltpu.make_async_copy(kernel_hbm, kernel_ref, small_sems.at[1])
    cot_copy = pltpu.make_async_copy(cot_hbm, cot_ref, small_sems.at[2])
    glu_copies = []
    for c, count in enumerate(CHUNKS):
        for half in range(2):
            columns = pl.ds(half * channels + sum(CHUNKS[:c]) * LANES, count * LANES)
            glu_copies.append(
                pltpu.make_async_copy(
                    glu_hbm.at[:, columns], glu_ref.at[:, columns], glu_sems.at[c, half]
                )
            )
    count_copy.start()
    kernel_copy.start()
    for copy in glu_copies:
        copy.start()
    cot_copy.start()
    count_copy.wait()
    counts = [count_ref[u] for u in range(UTT)]
    local_frames = sum(counts).astype(jnp.float32)
    stat_ref[...] = jnp.full(stat_ref.shape, local_frames, jnp.float32)
    for u in range(UTT):
        live_ref[pl.ds(u * SLOT, SLOT), :] = jnp.where(live_rows(counts[u]), 1.0, 0.0)
    kernel_copy.wait()
    for i in range(tiles):
        rows = kernel_ref[0, :, i * LANES : (i + 1) * LANES].astype(jnp.float32)
        rows = [rows[SUB * j : SUB * (j + 1)] for j in range(K // SUB)]
        for n, combo in enumerate(COMBOS):
            taps_ref[i, n] = added([rows[j] for j in combo])

    def tile(i, carry):
        lanes = lane_tile(i)
        gate_lanes = lane_tile(i + tiles)
        edge = jnp.zeros((HALF, LANES), jnp.float32)
        field_sum = jnp.zeros((SUB, LANES), jnp.float32)
        head = edge
        tail = edge
        total = jnp.zeros((SUB, LANES), jnp.float32)
        for u in range(UTT):
            rows = pl.ds(u * SLOT, SLOT)
            base = u * PADDED
            value = glu_ref[rows, lanes].astype(jnp.float32)
            gate = glu_ref[rows, gate_lanes].astype(jnp.float32)
            field = value * jax.nn.sigmoid(gate) * live_ref[rows, :]
            field_sum = field_sum + fold_rows(field)
            head = head + field[:HALF]
            field = jnp.concatenate([edge, field, edge], axis=0)
            near = field[: PADDED - SUB] - field[SUB:]
            field_ref[i, PLAIN, pl.ds(base, PADDED), :] = field
            field_ref[i, NEXT, pl.ds(base, PADDED - SUB), :] = near
            field_ref[i, SECOND, pl.ds(base, PADDED - 2 * SUB), :] = (
                field[: PADDED - 2 * SUB] - field[2 * SUB :]
            )
            field_ref[i, BOTH, pl.ds(base, PADDED - 3 * SUB), :] = (
                near[: PADDED - 3 * SUB] - near[2 * SUB :]
            )
            tail = tail + field_ref[i, PLAIN, pl.ds(base + counts[u], HALF), :]

        for u in range(UTT):
            base = u * PADDED

            def taps(step, sums):
                sums = list(sums)
                for r in range(R_STEP):
                    first = step * R_STEP + r
                    for n, product in enumerate(PRODUCTS):
                        tap = taps_ref[i, n, pl.ds(first, 1), :]
                        for m, field in enumerate(fields_at(field_ref, i, base + first, product)):
                            sums[4 * n + m] = sums[4 * n + m] + field * tap
                return tuple(sums)

            zero = jnp.zeros((SUB, LANES), jnp.float32)
            sums = lax.fori_loop(0, SUB // R_STEP, taps, (zero,) * (4 * len(PRODUCTS)))
            for m in range(SLOT // SUB // 4):
                for q, out in enumerate(combine(sums[m::4])):
                    at = pl.ds(u * SLOT + SUB * (4 * m + q), SUB)
                    conv_ref[i, at, :] = out
                    total = total + out * live_ref[at, :]
        local_mean = jnp.sum(total, axis=0, keepdims=True) / local_frames
        spread = jnp.zeros((SUB, LANES), jnp.float32)
        for u in range(UTT):
            rows = pl.ds(u * SLOT, SLOT)
            centered = (conv_ref[i, rows, :] - local_mean) * live_ref[rows, :]
            spread = spread + fold_rows(centered * centered)
        stat_ref[pl.ds(i, 1), :] = local_mean
        stat_ref[pl.ds(i + tiles, 1), :] = jnp.sum(spread, axis=0, keepdims=True)
        live_sum_ref[i] = jnp.sum(field_sum, axis=0, keepdims=True) - jnp.concatenate(
            [scan_rows(tail, True), scan_rows(head, False) - head], axis=0
        )
        return carry

    for c, count in enumerate(CHUNKS):
        glu_copies[2 * c].wait()
        glu_copies[2 * c + 1].wait()
        lax.fori_loop(sum(CHUNKS[:c]), sum(CHUNKS[: c + 1]), tile, 0, unroll=UNROLL)
    cot_copy.wait()


def merge_stats(parts, tiles):
    frames = added([part[2 * tiles : 2 * tiles + 1] for part in parts])
    mean = added([part[:tiles] * part[2 * tiles : 2 * tiles + 1] for part in parts]) / frames
    spread = added(
        [
            part[tiles : 2 * tiles]
            + part[2 * tiles : 2 * tiles + 1] * (part[:tiles] - mean) * (part[:tiles] - mean)
            for part in parts
        ]
    )
    return frames, mean, spread


def pair_kernel(tiles, own_ref, other_ref, out_ref):
    frames, mean, spread = merge_stats([own_ref[...], other_ref[...]], tiles)
    rest = jnp.broadcast_to(frames, (STAT_ROWS - 2 * tiles, LANES))
    for peer in range(out_ref.shape[0]):
        out_ref[peer, pl.ds(0, tiles), :] = mean
        out_ref[peer, pl.ds(tiles, tiles), :] = spread
        out_ref[peer, pl.ds(2 * tiles, STAT_ROWS - 2 * tiles), :] = rest


def back_kernel(
    stat_ref,
    own_ref,
    cot_ref,
    param_ref,
    field_ref,
    conv_ref,
    live_sum_ref,
    live_ref,
    out_ref,
    mean_ref,
    inv_ref,
    par_ref,
    tap_ref,
):
    tiles = conv_ref.shape[0]
    channels = tiles * LANES
    frames, mean, spread = merge_stats([stat_ref[p] for p in range(stat_ref.shape[0])], tiles)
    mean_ref[pl.ds(0, tiles), :] = mean
    inv_ref[pl.ds(0, tiles), :] = lax.rsqrt(spread / frames + eps_norm)
    par_ref[...] = param_ref[0].astype(jnp.float32)
    local_frames = own_ref[pl.ds(2 * tiles, 1), :]

    def tile(i):
        lanes = lane_tile(i)
        mean_row = mean_ref[pl.ds(i, 1), :]
        inv_row = inv_ref[pl.ds(i, 1), :]
        gain_row = par_ref[pl.ds(0, 1), lanes]
        shift_row = par_ref[pl.ds(1, 1), lanes]
        gain_sum = jnp.zeros((SUB, LANES), jnp.float32)
        shift_sum = jnp.zeros((SUB, LANES), jnp.float32)
        for u in range(UTT):
            rows = pl.ds(u * SLOT, SLOT)
            base = u * PADDED
            live = live_ref[rows, :]
            normed = (conv_ref[i, rows, :] - mean_row) * inv_row
            norm_out = gain_row * normed + shift_row
            sig = jax.nn.sigmoid(norm_out)
            slope = sig * (1.0 + norm_out * (1.0 - sig))
            upstream = cot_ref[rows, lanes].astype(jnp.float32) * slope * live
            normed = normed * live
            gain_sum = gain_sum + fold_rows(upstream * normed)
            shift_sum = shift_sum + fold_rows(upstream)
            for which, source in enumerate((upstream, normed)):
                blocks = [source[SUB * q : SUB * (q + 1)] for q in range(SLOT // SUB)]
                mixes = [
                    [added([blocks[4 * m + q] for q in combo]) for m in range(SLOT // SUB // 4)]
                    for combo in COMBOS
                ]

                def taps(step, carry):
                    for r in range(R_STEP):
                        first = step * R_STEP + r
                        parts = []
                        for mix, product in zip(mixes, PRODUCTS):
                            fields = fields_at(field_ref, i, base + first, product)
                            parts.append(added([x * field for x, field in zip(mix, fields)]))
                        for j, out in enumerate(combine(parts)):
                            at = pl.ds(SUB * (which * K + first + SUB * j), SUB)
                            tap_ref[at, :] = out if u == 0 else tap_ref[at, :] + out
                    return carry

                lax.fori_loop(0, SUB // R_STEP, taps, 0)
        scale = gain_row * inv_row
        tap_rows = added([tap_ref[pl.ds(row, 2 * K, stride=SUB), :] for row in range(SUB)])
        row = lax.broadcasted_iota(jnp.int32, (K, LANES), 0)
        extra = jnp.where(row == 0, jnp.sum(gain_sum, axis=0, keepdims=True), local_frames)
        extra = jnp.where(row == 1, jnp.sum(shift_sum, axis=0, keepdims=True), extra)
        block = jnp.concatenate(
            [tap_rows[:K] * scale, live_sum_ref[i] * scale, tap_rows[K:] * scale, extra], axis=0
        )
        return block.T

    core = lax.rem(lax.axis_index("dp"), 2)
    share = channels // (2 * out_ref.shape[1])
    pairs = TILE_RUN * LANES // share // 2

    def run(step, carry):
        turned = jnp.concatenate([tile(step * TILE_RUN + n) for n in range(TILE_RUN)], axis=0)
        for j in range(2 * pairs):
            side = core if j % 2 == 0 else 1 - core
            out_ref[side, step * pairs + j // 2] = turned[j * share : (j + 1) * share]
        return carry

    lax.fori_loop(0, tiles // TILE_RUN, run, 0)


def delta_kernel(sum_ref, drift_ref, drift_norm_ref, out_ref):
    share = sum_ref.shape[1]
    channels = drift_ref.shape[2]
    total = added([sum_ref[p] for p in range(sum_ref.shape[0])])
    frames = total[:, 3 * K + 2 : 3 * K + 3]
    gain_sum = total[:, 3 * K : 3 * K + 1]
    shift_sum = total[:, 3 * K + 1 : 3 * K + 2]
    live_part = pltpu.roll(total, LANES - K, 1)
    norm_part = pltpu.roll(total, LANES - 2 * K, 1)
    kernel_sum = total - (shift_sum * live_part + gain_sum * norm_part) / frames
    start = lax.axis_index("dp") * share
    first = jnp.minimum(start // LANES, channels // LANES - 2)
    window = pl.ds(pl.multiple_of(first * LANES, LANES), 2 * LANES)
    drift = jnp.concatenate(
        [
            drift_ref[0, :, window].astype(jnp.float32),
            drift_norm_ref[0, :, window].astype(jnp.float32),
            jnp.zeros((LANES - K - 2, 2 * LANES), jnp.float32),
        ],
        axis=0,
    )
    drift = pltpu.roll(drift, lax.rem(2 * LANES - (start - first * LANES), 2 * LANES), 1)
    drift = drift[:, :LANES].T[:share]
    lane = lax.broadcasted_iota(jnp.int32, (share, LANES), 1)
    norm_at = pltpu.roll(total, LANES - 2 * K, 1)
    sums = jnp.where(lane < K, kernel_sum, norm_at)
    delta = (drift + (grad_factor_base / frames) * sums).astype(jnp.bfloat16).astype(jnp.float32)
    weighted = delta * frames
    block = share // 3
    lane = lane[:block]
    packed = jnp.broadcast_to(frames[:block], (block, LANES))
    for b in range(3):
        piece = weighted[b * block : (b + 1) * block]
        moved = pltpu.roll(piece, b * K, 1) if b else piece
        packed = jnp.where((lane >= b * K) & (lane < (b + 1) * K), moved, packed)
        at = 3 * K + 2 * b
        moved = pltpu.roll(piece, at - K, 1)
        packed = jnp.where((lane >= at) & (lane < at + 2), moved, packed)
    for peer in range(out_ref.shape[0]):
        out_ref[peer] = packed


def average_kernel(sum_ref, kernel_ref, norm_ref):
    total = added([sum_ref[p] for p in range(sum_ref.shape[0])])
    block = total.shape[0]
    average = total / total[:, 3 * K + 6 : 3 * K + 7]
    average = jnp.concatenate([average, jnp.zeros((LANES - block, LANES), jnp.float32)], axis=0)
    turned = average.T
    for b in range(3):
        kernel_ref[:, b * block : (b + 1) * block] = turned[b * K : (b + 1) * K, :block]
        norm_ref[:, b * block : (b + 1) * block] = turned[3 * K + 2 * b : 3 * K + 2 * b + 2, :block]


VMEM_SPEC = pl.BlockSpec(memory_space=pltpu.VMEM)
HBM_SPEC = pl.BlockSpec(memory_space=pltpu.HBM)
PARAMS = pltpu.CompilerParams(vmem_limit_bytes=32 * 1024 * 1024)


def conv_stage(frame_count, glu_in, kernel, cotangent):
    tiles = cotangent.shape[1] // LANES
    far = [
        pltpu.with_memory_space_constraint(x, pltpu.HBM)
        for x in (frame_count, glu_in, kernel, cotangent)
    ]
    return pl.pallas_call(
        conv_kernel,
        out_shape=(
            jax.ShapeDtypeStruct((tiles, 4, UTT * PADDED, LANES), jnp.float32),
            jax.ShapeDtypeStruct((tiles, ROWS, LANES), jnp.float32),
            jax.ShapeDtypeStruct((STAT_ROWS, LANES), jnp.float32),
            jax.ShapeDtypeStruct(cotangent.shape, cotangent.dtype),
            jax.ShapeDtypeStruct((tiles, K, LANES), jnp.float32),
            jax.ShapeDtypeStruct((ROWS, LANES), jnp.float32),
        ),
        in_specs=[HBM_SPEC] * 4,
        out_specs=(VMEM_SPEC,) * 6,
        scratch_shapes=[
            pltpu.SMEM((UTT,), jnp.int32),
            pltpu.VMEM(glu_in.shape, glu_in.dtype),
            pltpu.VMEM(kernel.shape, kernel.dtype),
            pltpu.VMEM((tiles, len(PRODUCTS), SUB, LANES), jnp.float32),
            pltpu.SemaphoreType.DMA((3,)),
            pltpu.SemaphoreType.DMA((len(CHUNKS), 2)),
        ],
        compiler_params=PARAMS,
        name="conv_stats",
    )(*far)


def pair_stage(stats, other, peers, tiles):
    return pl.pallas_call(
        functools.partial(pair_kernel, tiles),
        out_shape=jax.ShapeDtypeStruct((peers, STAT_ROWS, LANES), jnp.float32),
        in_specs=[VMEM_SPEC] * 2,
        out_specs=VMEM_SPEC,
        compiler_params=PARAMS,
        name="pair_stats",
    )(stats, other)


def back_stage(gathered, stats, cotangent, norm_params, fields, conv_out, live_sum, live):
    channels = cotangent.shape[1]
    peers = gathered.shape[0]
    return pl.pallas_call(
        back_kernel,
        out_shape=jax.ShapeDtypeStruct((2, peers, channels // (2 * peers), LANES), jnp.float32),
        in_specs=[VMEM_SPEC] * 8,
        out_specs=VMEM_SPEC,
        scratch_shapes=[
            pltpu.VMEM((16, LANES), jnp.float32),
            pltpu.VMEM((16, LANES), jnp.float32),
            pltpu.VMEM((2, channels), jnp.float32),
            pltpu.VMEM((2 * K * SUB, LANES), jnp.float32),
        ],
        compiler_params=PARAMS,
        name="tap_sums",
    )(gathered, stats, cotangent, norm_params, fields, conv_out, live_sum, live)


def on_device(glu_in, cotangent, frame_count, kernel, norm_params, drift_kernel, drift_norm):
    channels = cotangent.shape[1]
    tiles = channels // LANES
    n_dp = lax.axis_size("dp")
    n_group = lax.axis_size("group")
    peers = n_dp // 2
    share = channels // n_dp
    same_core = [[2 * p + core for p in range(peers)] for core in range(2)]
    swap = [(i, i ^ 1) for i in range(n_dp)]

    fields, conv_out, stats, cot_near, live_sum, live = conv_stage(
        frame_count, glu_in, kernel, cotangent
    )
    other = lax.ppermute(stats, "dp", swap)
    spread_out = pair_stage(stats, other, peers, tiles)
    gathered = lax.all_to_all(spread_out, "dp", 0, 0, axis_index_groups=same_core)

    both = back_stage(gathered, stats, cot_near, norm_params, fields, conv_out, live_sum, live)
    arrived = lax.ppermute(both[1], "dp", swap)
    tap_sums = lax.all_to_all(both[0] + arrived, "dp", 0, 0, axis_index_groups=same_core)

    weighted = pl.pallas_call(
        delta_kernel,
        out_shape=jax.ShapeDtypeStruct((n_group, share // 3, LANES), jnp.float32),
        in_specs=[VMEM_SPEC] * 3,
        out_specs=VMEM_SPEC,
        compiler_params=PARAMS,
        name="group_delta",
    )(tap_sums, drift_kernel, drift_norm)
    weighted = lax.all_to_all(weighted, "group", 0, 0)

    return pl.pallas_call(
        average_kernel,
        out_shape=(
            jax.ShapeDtypeStruct((K, share), jnp.float32),
            jax.ShapeDtypeStruct((2, share), jnp.float32),
        ),
        in_specs=[VMEM_SPEC],
        out_specs=(VMEM_SPEC, VMEM_SPEC),
        compiler_params=PARAMS,
        name="group_average",
    )(weighted)


def solution(mesh):
    placed = (
        P(("dp", "group"), None),
        P(("dp", "group"), None),
        P(("dp", "group")),
        P("group", None, None),
        P("group", None, None),
        P("group", None, None),
        P("group", None, None),
    )
    return jax.shard_map(
        on_device,
        mesh=mesh,
        in_specs=placed,
        out_specs=(P(None, "dp"), P(None, "dp")),
        check_vma=False,
    )
```

time: 92.7 us -> 81.3 us (0.88)
  Pallas kernels: 21.3 us -> 12.9 us
  local copies, waits for them, and re-layouts: 3 us -> 0.04 us
    pallas_call x3, Pallas kernels: 20.1 us -> 11.8 us  [the longest x1 7.03 us: back_stage(): pl.pallas_call(back_kernel, out_shape=jax.ShapeDtypeStruct((2, peers, cha...]
    unnamed x16 -> x6, local copies, waits for them, and re-layouts: 2.97 us -> 0.02 us
where the time goes in v2:
time: 81.3 us; the launch traced here: 81 us
  blocking collectives  60.6 us (75%)
  Pallas kernels  12.9 us (16%)
  starting transfers between devices  3.84 us (5%)
  waiting for transfers between devices  2.84 us (3%)
    all_to_all x1, blocking collectives, on_device(): lax.all_to_all(spread_out, 'dp', 0, 0, axis_index_groups=same_core)  21.1 us
    all_to_all x1, blocking collectives, on_device(): weighted = lax.all_to_all(weighted, 'group', 0, 0)  21.1 us
    all_to_all x1, blocking collectives, on_device(): lax.all_to_all(both[0] + arrived, 'dp', 0, 0, axis_index_groups=same_core)  18.4 us
    pallas_call x1, Pallas kernels, back_stage(): pl.pallas_call(back_kernel, out_shape=jax.ShapeDtypeStruct((2, peers, cha...  7.03 us
    pallas_call x1, Pallas kernels, conv_stage(): pl.pallas_call(conv_kernel, out_shape=(jax.ShapeDtypeStruct((tiles, 4, UT...  4.71 us
    ppermute x1, starting transfers between devices, on_device(): other = lax.ppermute(stats, 'dp', swap)  1.92 us
    ppermute x1, starting transfers between devices, on_device(): arrived = lax.ppermute(both[1], 'dp', swap)  1.92 us
    ppermute x1, waiting for transfers between devices, on_device(): arrived = lax.ppermute(both[1], 'dp', swap)  1.69 us
  transfers between devices with their start and end apart: 2, of which 2 were waited for; matrix products, arithmetic and copies ran while one was open for 0% of the time, Pallas kernels for 0%

profile of v2, /device:TPU:2, one launch (start us, length us, event | category | flops | bytes accessed | tf_op | source)
XLA Modules:
  0.0 81.0 jit_solution(3623061560054049742)
XLA Ops:
  0.6 0.0 copy-start.1
  0.6 4.7 %conv_stats.1 = (f32[12,4,320,128]{3,2,1,0:T(8,128)S(1)}, f32[12,256,128]{2,1,0:T(8,128)S(1)}, f32[32,128]{1,0:T(8,128)S(1)}, bf16[256,1536]{1,0:T(8,128)(2,1)S(...) custom-call(s32[2]{0:T(128)} %count_hbm.1, bf16[256,3072]{1,0:T(8,128)(2,1)} %glu_hbm.1, ...), custom_call_target="tpu_custom_call" | custom-call | tf_op jit(solution)/shard_map/conv_stats/pallas_call | solution.py:382
  5.4 1.9 %collective-permute-start = (f32[32,128]{1,0:T(8,128)S(1)}, f32[32,128]{1,0:T(8,128)S(1)}, u32[]{:S(2)}, u32[]{:S(2)}) collective-permute-start(f32[32,128]{1,0:T(8,128)S(1)} %get-tuple-element.8.own_ref), channel_id=1, source_target_pairs={{0,16},{16,0},{32,48},{48,32},{64,80},{80,64},{96,112},{112,96},{1... | collective-permute-start | bytes 49160 | tf_op jit(solution)/shard_map/ppermute | solution.py:450
  7.3 1.1 %collective-permute-done.other_ref = f32[32,128]{1,0:T(8,128)S(1)} collective-permute-done((f32[32,128]{1,0:T(8,128)S(1)}, f32[32,128]{1,0:T(8,128)S(1)}, u32[]{:S(2)}, u32[]{:S(2)}) %collective-permute-start) | collective-permute-done | bytes 16416 | tf_op jit(solution)/shard_map/ppermute | solution.py:450
  8.5 21.1 %all_to_all.15.stat_ref = f32[16,32,128]{2,1,0:T(8,128)S(1)} all-to-all(f32[16,32,128]{2,1,0:T(8,128)S(1)} %pair_stats.1), channel_id=1, replica_groups={{0,32,64,96,128,160,192,224,256,288,320,352,384,416,448,480},{16,48,80,..., dimensions={0} | all-to-all | bytes 524288 | tf_op jit(solution)/shard_map/all_to_all | solution.py:452
  29.6 0.0 copy-done.1
  29.6 7.0 %tap_sums.1 = f32[2,16,48,128]{3,2,1,0:T(8,128)S(1)} custom-call(f32[16,32,128]{2,1,0:T(8,128)S(1)} %all_to_all.15.stat_ref, f32[32,128]{1,0:T(8,128)S(1)} %get-tuple-element.8.own_ref, bf16[256,1536]{1,0:T(8,128)(2,1)S(1)} %get-tuple-element.9.cot_ref, bf16[1,2,1536]{2,1,0:T(2,128)(2,1)S(1)} %copy-done.1, ...), custom_call_target="tpu_custom_call" | custom-call | tf_op jit(solution)/shard_map/tap_sums/pallas_call | solution.py:421
  36.6 0.0 copy-start
  36.6 0.0 copy-start.2
  36.7 1.9 %collective-permute-start.1 = (f32[16,48,128]{2,1,0:T(8,128)S(1)}, f32[16,48,128]{2,1,0:T(8,128)S(1)}, u32[]{:S(2)}, u32[]{:S(2)}) collective-permute-start(f32[16,48,128]{2,1,0:T(8,128)S(1)} %slice_bitcast_fusion), channel_id=1, source_target_pairs={{0,16},{16,0},{32,48},{48,32},{64,80},{80,64},{96,112},{112,96},{1... | collective-permute-start | bytes 1179656 | tf_op jit(solution)/shard_map/ppermute | solution.py:455
  38.6 1.7 %collective-permute-done.1 = f32[16,48,128]{2,1,0:T(8,128)S(1)} collective-permute-done((f32[16,48,128]{2,1,0:T(8,128)S(1)}, f32[16,48,128]{2,1,0:T(8,128)S(1)}, u32[]{:S(2)}, u32[]{:S(2)}) %collective-permute-start.1) | collective-permute-done | bytes 393248 | tf_op jit(solution)/shard_map/ppermute | solution.py:455
  40.4 18.4 %all_to_all.16.sum_ref = f32[16,48,128]{2,1,0:T(8,128)S(1)} all-to-all(f32[16,48,128]{2,1,0:T(8,128)S(1)} %fusion), channel_id=1, replica_groups={{0,32,64,96,128,160,192,224,256,288,320,352,384,416,448,480},{16,48,80,..., dimensions={0} | all-to-all | bytes 786432 | tf_op jit(solution)/shard_map/all_to_all | solution.py:456
  58.7 0.0 copy-done
  58.7 0.0 copy-done.2
  58.7 0.3 group_delta.1
  59.0 21.1 %all_to_all.17.sum_ref = f32[16,16,128]{2,1,0:T(8,128)S(1)} all-to-all(f32[16,16,128]{2,1,0:T(8,128)S(1)} %group_delta.1), channel_id=1, replica_groups=mesh['dp'=32,'group'=16] {'group'}, dimensions={0} | all-to-all | bytes 262144 | tf_op jit(solution)/shard_map/all_to_all | solution.py:466
  80.1 0.9 %group_average.1 = (f32[32,48]{1,0:T(8,128)}, f32[2,48]{1,0:T(2,128)}) custom-call(f32[16,16,128]{2,1,0:T(8,128)S(1)} %all_to_all.17.sum_ref), custom_call_target="tpu_custom_call" | custom-call | tf_op jit(solution)/shard_map/group_average/pallas_call | solution.py:468
  (3 shorter events, 0.1 us)
Async XLA Ops:
  0.6 29.0 %copy-start.1 = (bf16[1,2,1536]{2,1,0:T(2,128)(2,1)S(1)}, bf16[1,2,1536]{2,1,0:T(2,128)(2,1)}, u32[]{:S(2)}) copy-start(bf16[1,2,1536]{2,1,0:T(2,128)(2,1)} %param_ref.1) | copy-start | bytes 18436
  5.4 3.1 %collective-permute-start = (f32[32,128]{1,0:T(8,128)S(1)}, f32[32,128]{1,0:T(8,128)S(1)}, u32[]{:S(2)}, u32[]{:S(2)}) collective-permute-start(f32[32,128]{1,0:T(8,128)S(1)} %get-tuple-element.8.own_ref), channel_id=1, source_target_pairs={{0,16},{16,0},{32,48},{48,32},{64,80},{80,64},{96,112},{112,96},{1... | collective-permute-start | bytes 49160 | tf_op jit(solution)/shard_map/ppermute | solution.py:450
  36.6 22.1 %copy-start = (bf16[1,32,1536]{2,1,0:T(8,128)(2,1)S(1)}, bf16[1,32,1536]{2,1,0:T(8,128)(2,1)}, u32[]{:S(2)}) copy-start(bf16[1,32,1536]{2,1,0:T(8,128)(2,1)} %drift_ref.1) | copy-start | bytes 294916
  36.6 22.1 %copy-start.2 = (bf16[1,2,1536]{2,1,0:T(2,128)(2,1)S(1)}, bf16[1,2,1536]{2,1,0:T(2,128)(2,1)}, u32[]{:S(2)}) copy-start(bf16[1,2,1536]{2,1,0:T(2,128)(2,1)} %drift_norm_ref.1) | copy-start | bytes 18436
  36.7 3.6 %collective-permute-start.1 = (f32[16,48,128]{2,1,0:T(8,128)S(1)}, f32[16,48,128]{2,1,0:T(8,128)S(1)}, u32[]{:S(2)}, u32[]{:S(2)}) collective-permute-start(f32[16,48,128]{2,1,0:T(8,128)S(1)} %slice_bitcast_fusion), channel_id=1, source_target_pairs={{0,16},{16,0},{32,48},{48,32},{64,80},{80,64},{96,112},{112,96},{1... | collective-permute-start | bytes 1179656 | tf_op jit(solution)/shard_map/ppermute | solution.py:455

commit v3 on v2

--- a/solution.py
+++ b/solution.py
@@ -16,7 +16,6 @@
 UTT = 2
 ROWS = UTT * SLOT
 PADDED = HALF + SLOT + HALF
-STAT_ROWS = 32
 CHUNKS = (4, 8)
 R_STEP = 8
 UNROLL = 4
@@ -28,6 +27,10 @@
 
 def lane_tile(i):
     return pl.ds(pl.multiple_of(i * LANES, LANES), LANES)
+
+
+def peer_rows(row, peers, tiles):
+    return pl.ds(row, peers, stride=2 * tiles + 1)
 
 
 def live_rows(count):
@@ -206,26 +209,69 @@
     cot_copy.wait()
 
 
-def merge_stats(parts, tiles):
-    frames = added([part[2 * tiles : 2 * tiles + 1] for part in parts])
-    mean = added([part[:tiles] * part[2 * tiles : 2 * tiles + 1] for part in parts]) / frames
+def pair_kernel(own_ref, other_ref, out_ref):
+    rows = own_ref.shape[0] - SUB + 1
+    tiles = rows // 2
+    parts = [ref[...] for ref in (own_ref, other_ref)]
+    counts = [part[2 * tiles : 2 * tiles + 1] for part in parts]
+    frames = counts[0] + counts[1]
+    means = [part[:tiles] for part in parts]
+    mean = (counts[0] * means[0] + counts[1] * means[1]) / frames
     spread = added(
-        [
-            part[tiles : 2 * tiles]
-            + part[2 * tiles : 2 * tiles + 1] * (part[:tiles] - mean) * (part[:tiles] - mean)
-            for part in parts
-        ]
-    )
-    return frames, mean, spread
-
-
-def pair_kernel(tiles, own_ref, other_ref, out_ref):
-    frames, mean, spread = merge_stats([own_ref[...], other_ref[...]], tiles)
-    rest = jnp.broadcast_to(frames, (STAT_ROWS - 2 * tiles, LANES))
-    for peer in range(out_ref.shape[0]):
-        out_ref[peer, pl.ds(0, tiles), :] = mean
-        out_ref[peer, pl.ds(tiles, tiles), :] = spread
-        out_ref[peer, pl.ds(2 * tiles, STAT_ROWS - 2 * tiles), :] = rest
+        [part[tiles : 2 * tiles] + n * (m - mean) * (m - mean) for part, n, m in zip(parts, counts, means)]
+    )
+    merged = jnp.concatenate([mean, spread, jnp.broadcast_to(frames, (SUB, LANES))], axis=0)
+    for peer in range(out_ref.shape[0] // rows):
+        out_ref[pl.ds(peer * rows, rows), :] = merged[:rows]
+
+
+def store_taps(tap_ref, field_ref, i, u, source):
+    blocks = [source[SUB * q : SUB * (q + 1)] for q in range(SLOT // SUB)]
+    mixes = [
+        [added([blocks[4 * m + q] for q in combo]) for m in range(SLOT // SUB // 4)]
+        for combo in COMBOS
+    ]
+    for first in range(SUB):
+        parts = []
+        for mix, product in zip(mixes, PRODUCTS):
+            fields = fields_at(field_ref, i, u * PADDED + first, product)
+            parts.append(added([x * field for x, field in zip(mix, fields)]))
+        for j, out in enumerate(combine(parts)):
+            at = pl.ds(SUB * (first + SUB * j), SUB)
+            tap_ref[at, :] = out if u == 0 else tap_ref[at, :] + out
+
+
+def load_taps(tap_ref):
+    return added([tap_ref[pl.ds(row, K, stride=SUB), :] for row in range(SUB)])
+
+
+def lane_in(low, high):
+    lane = lax.broadcasted_iota(jnp.int32, (SUB, LANES), 1)
+    return (lane >= low) & (lane < high)
+
+
+def pack_chunk(chunk):
+    blocks = [chunk[SUB * b : SUB * (b + 1)] for b in range(6)]
+    last = pltpu.roll(blocks[5], 3 * K, 1)
+    moved = [pltpu.roll(blocks[4], (3 - n) * K, 1) for n in range(3)] + [last]
+    packed = [jnp.where(lane_in(0, 3 * K), blocks[n], moved[n]) for n in range(4)]
+    for b in range(6):
+        extra = pltpu.roll(blocks[b], LANES - K + 2 * b, 1)
+        last = jnp.where(lane_in(2 * K + 2 * b, 2 * K + 2 * b + 3), extra, last)
+    return packed + [last]
+
+
+def unpack_chunk(packed):
+    parts = [packed[SUB * n : SUB * (n + 1)] for n in range(5)]
+    four = pltpu.roll(parts[0], K, 1)
+    four = jnp.where(lane_in(K, 2 * K), pltpu.roll(parts[1], 2 * K, 1), four)
+    four = jnp.where(lane_in(2 * K, 3 * K), pltpu.roll(parts[2], 3 * K, 1), four)
+    five = jnp.where(lane_in(0, K), pltpu.roll(parts[3], K, 1), pltpu.roll(parts[4], K, 1))
+    sums = jnp.concatenate(parts[:4] + [four, five], axis=0)
+    at = [2 * K + 2 * b for b in range(6)]
+    gain_sum = jnp.concatenate([parts[4][:, n : n + 1] for n in at], axis=0)
+    shift_sum = jnp.concatenate([parts[4][:, n + 1 : n + 2] for n in at], axis=0)
+    return sums, gain_sum, shift_sum, parts[4][:1, at[5] + 2 : at[5] + 3]
 
 
 def back_kernel(
@@ -238,30 +284,35 @@
     live_sum_ref,
     live_ref,
     out_ref,
-    mean_ref,
-    inv_ref,
     par_ref,
-    tap_ref,
+    up_ref,
+    norm_ref,
 ):
     tiles = conv_ref.shape[0]
-    channels = tiles * LANES
-    frames, mean, spread = merge_stats([stat_ref[p] for p in range(stat_ref.shape[0])], tiles)
-    mean_ref[pl.ds(0, tiles), :] = mean
-    inv_ref[pl.ds(0, tiles), :] = lax.rsqrt(spread / frames + eps_norm)
+    pairs = out_ref.shape[1]
+    share = tiles * LANES // (2 * pairs)
+    per_run = TILE_RUN * LANES // share
+    core = lax.rem(lax.axis_index("dp"), 2)
     par_ref[...] = param_ref[0].astype(jnp.float32)
     local_frames = own_ref[pl.ds(2 * tiles, 1), :]
+    counts = stat_ref[peer_rows(2 * tiles, pairs, tiles), :]
+    frames = jnp.sum(counts, axis=0, keepdims=True)
+    row = lax.broadcasted_iota(jnp.int32, (SUB, LANES), 0)
+    rest = jnp.zeros((K - SUB, LANES), jnp.float32)
 
     def tile(i):
         lanes = lane_tile(i)
-        mean_row = mean_ref[pl.ds(i, 1), :]
-        inv_row = inv_ref[pl.ds(i, 1), :]
+        means = stat_ref[peer_rows(i, pairs, tiles), :]
+        mean_row = jnp.sum(counts * means, axis=0, keepdims=True) / frames
+        apart = means - mean_row
+        spread = stat_ref[peer_rows(i + tiles, pairs, tiles), :] + counts * apart * apart
+        inv_row = lax.rsqrt(jnp.sum(spread, axis=0, keepdims=True) / frames + eps_norm)
         gain_row = par_ref[pl.ds(0, 1), lanes]
         shift_row = par_ref[pl.ds(1, 1), lanes]
         gain_sum = jnp.zeros((SUB, LANES), jnp.float32)
         shift_sum = jnp.zeros((SUB, LANES), jnp.float32)
         for u in range(UTT):
             rows = pl.ds(u * SLOT, SLOT)
-            base = u * PADDED
             live = live_ref[rows, :]
             normed = (conv_ref[i, rows, :] - mean_row) * inv_row
             norm_out = gain_row * normed + shift_row
@@ -271,57 +322,41 @@
             normed = normed * live
             gain_sum = gain_sum + fold_rows(upstream * normed)
             shift_sum = shift_sum + fold_rows(upstream)
-            for which, source in enumerate((upstream, normed)):
-                blocks = [source[SUB * q : SUB * (q + 1)] for q in range(SLOT // SUB)]
-                mixes = [
-                    [added([blocks[4 * m + q] for q in combo]) for m in range(SLOT // SUB // 4)]
-                    for combo in COMBOS
-                ]
-
-                def taps(step, carry):
-                    for r in range(R_STEP):
-                        first = step * R_STEP + r
-                        parts = []
-                        for mix, product in zip(mixes, PRODUCTS):
-                            fields = fields_at(field_ref, i, base + first, product)
-                            parts.append(added([x * field for x, field in zip(mix, fields)]))
-                        for j, out in enumerate(combine(parts)):
-                            at = pl.ds(SUB * (which * K + first + SUB * j), SUB)
-                            tap_ref[at, :] = out if u == 0 else tap_ref[at, :] + out
-                    return carry
-
-                lax.fori_loop(0, SUB // R_STEP, taps, 0)
+            store_taps(up_ref, field_ref, i, u, upstream)
+            store_taps(norm_ref, field_ref, i, u, normed)
         scale = gain_row * inv_row
-        tap_rows = added([tap_ref[pl.ds(row, 2 * K, stride=SUB), :] for row in range(SUB)])
-        row = lax.broadcasted_iota(jnp.int32, (K, LANES), 0)
         extra = jnp.where(row == 0, jnp.sum(gain_sum, axis=0, keepdims=True), local_frames)
         extra = jnp.where(row == 1, jnp.sum(shift_sum, axis=0, keepdims=True), extra)
         block = jnp.concatenate(
-            [tap_rows[:K] * scale, live_sum_ref[i] * scale, tap_rows[K:] * scale, extra], axis=0
+            [
+                load_taps(up_ref) * scale,
+                live_sum_ref[i] * scale,
+                load_taps(norm_ref) * scale,
+                extra,
+                rest,
+            ],
+            axis=0,
         )
         return block.T
 
-    core = lax.rem(lax.axis_index("dp"), 2)
-    share = channels // (2 * out_ref.shape[1])
-    pairs = TILE_RUN * LANES // share // 2
-
     def run(step, carry):
         turned = jnp.concatenate([tile(step * TILE_RUN + n) for n in range(TILE_RUN)], axis=0)
-        for j in range(2 * pairs):
+        for j in range(per_run):
             side = core if j % 2 == 0 else 1 - core
-            out_ref[side, step * pairs + j // 2] = turned[j * share : (j + 1) * share]
+            chunk = turned[j * share : (j + 1) * share]
+            for n, part in enumerate(pack_chunk(chunk)):
+                out_ref[side, step * (per_run // 2) + j // 2, pl.ds(n * SUB, SUB), :] = part
         return carry
 
     lax.fori_loop(0, tiles // TILE_RUN, run, 0)
 
 
 def delta_kernel(sum_ref, drift_ref, drift_norm_ref, out_ref):
-    share = sum_ref.shape[1]
+    share = 6 * SUB
     channels = drift_ref.shape[2]
-    total = added([sum_ref[p] for p in range(sum_ref.shape[0])])
-    frames = total[:, 3 * K + 2 : 3 * K + 3]
-    gain_sum = total[:, 3 * K : 3 * K + 1]
-    shift_sum = total[:, 3 * K + 1 : 3 * K + 2]
+    total, gain_sum, shift_sum, frames = unpack_chunk(
+        added([sum_ref[p] for p in range(sum_ref.shape[0])])
+    )
     live_part = pltpu.roll(total, LANES - K, 1)
     norm_part = pltpu.roll(total, LANES - 2 * K, 1)
     kernel_sum = total - (shift_sum * live_part + gain_sum * norm_part) / frames
@@ -339,13 +374,12 @@
     drift = pltpu.roll(drift, lax.rem(2 * LANES - (start - first * LANES), 2 * LANES), 1)
     drift = drift[:, :LANES].T[:share]
     lane = lax.broadcasted_iota(jnp.int32, (share, LANES), 1)
-    norm_at = pltpu.roll(total, LANES - 2 * K, 1)
-    sums = jnp.where(lane < K, kernel_sum, norm_at)
+    sums = jnp.where(lane < K, kernel_sum, jnp.where(lane == K, gain_sum, shift_sum))
     delta = (drift + (grad_factor_base / frames) * sums).astype(jnp.bfloat16).astype(jnp.float32)
     weighted = delta * frames
     block = share // 3
     lane = lane[:block]
-    packed = jnp.broadcast_to(frames[:block], (block, LANES))
+    packed = jnp.broadcast_to(frames, (block, LANES))
     for b in range(3):
         piece = weighted[b * block : (b + 1) * block]
         moved = pltpu.roll(piece, b * K, 1) if b else piece
@@ -371,6 +405,10 @@
 VMEM_SPEC = pl.BlockSpec(memory_space=pltpu.VMEM)
 HBM_SPEC = pl.BlockSpec(memory_space=pltpu.HBM)
 PARAMS = pltpu.CompilerParams(vmem_limit_bytes=32 * 1024 * 1024)
+
+
+def cost(flops):
+    return pl.CostEstimate(flops=flops, bytes_accessed=0, transcendentals=0)
 
 
 def conv_stage(frame_count, glu_in, kernel, cotangent):
@@ -384,7 +422,7 @@
         out_shape=(
             jax.ShapeDtypeStruct((tiles, 4, UTT * PADDED, LANES), jnp.float32),
             jax.ShapeDtypeStruct((tiles, ROWS, LANES), jnp.float32),
-            jax.ShapeDtypeStruct((STAT_ROWS, LANES), jnp.float32),
+            jax.ShapeDtypeStruct((2 * tiles + SUB, LANES), jnp.float32),
             jax.ShapeDtypeStruct(cotangent.shape, cotangent.dtype),
             jax.ShapeDtypeStruct((tiles, K, LANES), jnp.float32),
             jax.ShapeDtypeStruct((ROWS, LANES), jnp.float32),
@@ -404,10 +442,10 @@
     )(*far)
 
 
-def pair_stage(stats, other, peers, tiles):
+def pair_stage(stats, other, pairs):
     return pl.pallas_call(
-        functools.partial(pair_kernel, tiles),
-        out_shape=jax.ShapeDtypeStruct((peers, STAT_ROWS, LANES), jnp.float32),
+        pair_kernel,
+        out_shape=jax.ShapeDtypeStruct((pairs * (stats.shape[0] - SUB + 1), LANES), jnp.float32),
         in_specs=[VMEM_SPEC] * 2,
         out_specs=VMEM_SPEC,
         compiler_params=PARAMS,
@@ -415,19 +453,17 @@
     )(stats, other)
 
 
-def back_stage(gathered, stats, cotangent, norm_params, fields, conv_out, live_sum, live):
-    channels = cotangent.shape[1]
-    peers = gathered.shape[0]
+def back_stage(gathered, stats, cotangent, norm_params, fields, conv_out, live_sum, live, pairs):
+    tiles = conv_out.shape[0]
     return pl.pallas_call(
         back_kernel,
-        out_shape=jax.ShapeDtypeStruct((2, peers, channels // (2 * peers), LANES), jnp.float32),
+        out_shape=jax.ShapeDtypeStruct((2, pairs, 5 * SUB, LANES), jnp.float32),
         in_specs=[VMEM_SPEC] * 8,
         out_specs=VMEM_SPEC,
         scratch_shapes=[
-            pltpu.VMEM((16, LANES), jnp.float32),
-            pltpu.VMEM((16, LANES), jnp.float32),
-            pltpu.VMEM((2, channels), jnp.float32),
-            pltpu.VMEM((2 * K * SUB, LANES), jnp.float32),
+            pltpu.VMEM((2, tiles * LANES), jnp.float32),
+            pltpu.VMEM((K * SUB, LANES), jnp.float32),
+            pltpu.VMEM((K * SUB, LANES), jnp.float32),
         ],
         compiler_params=PARAMS,
         name="tap_sums",
@@ -435,23 +471,22 @@
 
 
 def on_device(glu_in, cotangent, frame_count, kernel, norm_params, drift_kernel, drift_norm):
-    channels = cotangent.shape[1]
-    tiles = channels // LANES
     n_dp = lax.axis_size("dp")
     n_group = lax.axis_size("group")
-    peers = n_dp // 2
-    share = channels // n_dp
-    same_core = [[2 * p + core for p in range(peers)] for core in range(2)]
+    pairs = n_dp // 2
+    share = cotangent.shape[1] // n_dp
     swap = [(i, i ^ 1) for i in range(n_dp)]
+    same_core = [[2 * p + core for p in range(pairs)] for core in range(2)]
 
     fields, conv_out, stats, cot_near, live_sum, live = conv_stage(
         frame_count, glu_in, kernel, cotangent
     )
-    other = lax.ppermute(stats, "dp", swap)
-    spread_out = pair_stage(stats, other, peers, tiles)
-    gathered = lax.all_to_all(spread_out, "dp", 0, 0, axis_index_groups=same_core)
-
-    both = back_stage(gathered, stats, cot_near, norm_params, fields, conv_out, live_sum, live)
+    merged = pair_stage(stats, lax.ppermute(stats, "dp", swap), pairs)
+    gathered = lax.all_to_all(
+        merged.reshape(pairs, 1, -1), "dp", 0, 0, axis_index_groups=same_core
+    ).reshape(merged.shape)
+
+    both = back_stage(gathered, stats, cot_near, norm_params, fields, conv_out, live_sum, live, pairs)
     arrived = lax.ppermute(both[1], "dp", swap)
     tap_sums = lax.all_to_all(both[0] + arrived, "dp", 0, 0, axis_index_groups=same_core)
 

time: 81.3 us -> 78.3 us (0.963)
  blocking collectives: 60.6 us -> 58.2 us
    all_to_all x1, blocking collectives: 18.4 us -> 17 us  [on_device(): lax.all_to_all(both[0] + arrived, 'dp', 0, 0, axis_index_groups=same_core)]
    all_to_all x1, blocking collectives: 21.1 us -> 20 us  [on_device(): lax.all_to_all(merged.reshape(pairs, 1, -1), 'dp', 0, 0, axis_index_group...]
where the time goes in v3:
time: 78.3 us; the launch traced here: 78.1 us
  blocking collectives  58.2 us (74%)
  Pallas kernels  12.5 us (16%)
  starting transfers between devices  3.84 us (5%)
  waiting for transfers between devices  2.74 us (3%)
    all_to_all x1, blocking collectives, on_device(): weighted = lax.all_to_all(weighted, 'group', 0, 0)  21.1 us
    all_to_all x1, blocking collectives, on_device(): lax.all_to_all(merged.reshape(pairs, 1, -1), 'dp', 0, 0, axis_index_group...  20 us
    all_to_all x1, blocking collectives, on_device(): lax.all_to_all(both[0] + arrived, 'dp', 0, 0, axis_index_groups=same_core)  17 us
    pallas_call x1, Pallas kernels, back_stage(): pl.pallas_call(back_kernel, out_shape=jax.ShapeDtypeStruct((2, pairs, 5 *...  7.03 us
    pallas_call x1, Pallas kernels, conv_stage(): pl.pallas_call(conv_kernel, out_shape=(jax.ShapeDtypeStruct((tiles, 4, UT...  4.31 us
    ppermute x1, starting transfers between devices, on_device(): arrived = lax.ppermute(both[1], 'dp', swap)  1.92 us
    ppermute x1, starting transfers between devices, on_device(): merged = pair_stage(stats, lax.ppermute(stats, 'dp', swap), pairs)  1.92 us
    ppermute x1, waiting for transfers between devices, on_device(): arrived = lax.ppermute(both[1], 'dp', swap)  1.59 us
  transfers between devices with their start and end apart: 2, of which 2 were waited for; matrix products, arithmetic and copies ran while one was open for 0% of the time, Pallas kernels for 0%

profile of v3, /device:TPU:2, one launch (start us, length us, event | category | flops | bytes accessed | tf_op | source)
XLA Modules:
  0.0 78.1 jit_solution(2950058596530697915)
XLA Ops:
  0.6 0.0 copy-start.1
  0.6 4.3 %conv_stats.1 = (f32[12,4,320,128]{3,2,1,0:T(8,128)S(1)}, f32[12,256,128]{2,1,0:T(8,128)S(1)}, f32[32,128]{1,0:T(8,128)S(1)}, bf16[256,1536]{1,0:T(8,128)(2,1)S(...) custom-call(s32[2]{0:T(128)} %count_hbm.1, bf16[256,3072]{1,0:T(8,128)(2,1)} %glu_hbm.1, ...), custom_call_target="tpu_custom_call" | custom-call | tf_op jit(solution)/shard_map/conv_stats/pallas_call | solution.py:420
  5.0 1.9 %collective-permute-start = (f32[32,128]{1,0:T(8,128)S(1)}, f32[32,128]{1,0:T(8,128)S(1)}, u32[]{:S(2)}, u32[]{:S(2)}) collective-permute-start(f32[32,128]{1,0:T(8,128)S(1)} %get-tuple-element.8.own_ref), channel_id=1, source_target_pairs={{0,16},{16,0},{32,48},{48,32},{64,80},{80,64},{96,112},{112,96},{1... | collective-permute-start | bytes 49160 | tf_op jit(solution)/shard_map/ppermute | solution.py:484
  6.9 1.1 %collective-permute-done.other_ref = f32[32,128]{1,0:T(8,128)S(1)} collective-permute-done((f32[32,128]{1,0:T(8,128)S(1)}, f32[32,128]{1,0:T(8,128)S(1)}, u32[]{:S(2)}, u32[]{:S(2)}) %collective-permute-start) | collective-permute-done | bytes 16416 | tf_op jit(solution)/shard_map/ppermute | solution.py:484
  8.1 20.0 %all_to_all.15 = f32[16,1,3200]{2,1,0:T(1,128)S(1)} all-to-all(f32[16,1,3200]{2,1,0:T(1,128)S(1)} %bitcast.9), channel_id=1, replica_groups={{0,32,64,96,128,160,192,224,256,288,320,352,384,416,448,480},{16,48,80,..., dimensions={0} | all-to-all | bytes 409600 | tf_op jit(solution)/shard_map/all_to_all | solution.py:485
  28.1 0.0 copy-done.1
  28.1 7.0 %tap_sums.1 = f32[2,16,40,128]{3,2,1,0:T(8,128)S(1)} custom-call(f32[400,128]{1,0:T(8,128)S(1)} %bitcast.8, f32[32,128]{1,0:T(8,128)S(1)} %get-tuple-element.8.own_ref, bf16[256,1536]{1,0:T(8,128)(2,1)S(1)} %get-tuple-element.9.cot_ref, bf16[1,2,1536]{2,1,0:T(2,128)(2,1)S(1)} %copy-done.1, f32[12,4,320,128]{3,2,1,0:T(8,128)S(1)} %get-tuple-element.10.field_ref, ...), custom_call_target="tpu_custom_call" | custom-call | tf_op jit(solution)/shard_map/tap_sums/pallas_call | solution.py:458
  35.1 0.0 copy-start
  35.2 0.0 copy-start.2
  35.2 1.9 %collective-permute-start.1 = (f32[16,40,128]{2,1,0:T(8,128)S(1)}, f32[16,40,128]{2,1,0:T(8,128)S(1)}, u32[]{:S(2)}, u32[]{:S(2)}) collective-permute-start(f32[16,40,128]{2,1,0:T(8,128)S(1)} %slice_bitcast_fusion), channel_id=1, source_target_pairs={{0,16},{16,0},{32,48},{48,32},{64,80},{80,64},{96,112},{112,96},{1... | collective-permute-start | bytes 983048 | tf_op jit(solution)/shard_map/ppermute | solution.py:490
  37.1 1.6 %collective-permute-done.1 = f32[16,40,128]{2,1,0:T(8,128)S(1)} collective-permute-done((f32[16,40,128]{2,1,0:T(8,128)S(1)}, f32[16,40,128]{2,1,0:T(8,128)S(1)}, u32[]{:S(2)}, u32[]{:S(2)}) %collective-permute-start.1) | collective-permute-done | bytes 327712 | tf_op jit(solution)/shard_map/ppermute | solution.py:490
  38.8 17.0 %all_to_all.16.sum_ref = f32[16,40,128]{2,1,0:T(8,128)S(1)} all-to-all(f32[16,40,128]{2,1,0:T(8,128)S(1)} %fusion), channel_id=1, replica_groups={{0,32,64,96,128,160,192,224,256,288,320,352,384,416,448,480},{16,48,80,..., dimensions={0} | all-to-all | bytes 655360 | tf_op jit(solution)/shard_map/all_to_all | solution.py:491
  55.8 0.0 copy-done
  55.8 0.0 copy-done.2
  55.8 0.3 group_delta.1
  56.1 21.1 %all_to_all.17.sum_ref = f32[16,16,128]{2,1,0:T(8,128)S(1)} all-to-all(f32[16,16,128]{2,1,0:T(8,128)S(1)} %group_delta.1), channel_id=1, replica_groups=mesh['dp'=32,'group'=16] {'group'}, dimensions={0} | all-to-all | bytes 262144 | tf_op jit(solution)/shard_map/all_to_all | solution.py:501
  77.2 0.9 %group_average.1 = (f32[32,48]{1,0:T(8,128)}, f32[2,48]{1,0:T(2,128)}) custom-call(f32[16,16,128]{2,1,0:T(8,128)S(1)} %all_to_all.17.sum_ref), custom_call_target="tpu_custom_call" | custom-call | tf_op jit(solution)/shard_map/group_average/pallas_call | solution.py:503
  (3 shorter events, 0.1 us)
Async XLA Ops:
  0.6 27.5 %copy-start.1 = (bf16[1,2,1536]{2,1,0:T(2,128)(2,1)S(1)}, bf16[1,2,1536]{2,1,0:T(2,128)(2,1)}, u32[]{:S(2)}) copy-start(bf16[1,2,1536]{2,1,0:T(2,128)(2,1)} %param_ref.1) | copy-start | bytes 18436
  5.0 3.1 %collective-permute-start = (f32[32,128]{1,0:T(8,128)S(1)}, f32[32,128]{1,0:T(8,128)S(1)}, u32[]{:S(2)}, u32[]{:S(2)}) collective-permute-start(f32[32,128]{1,0:T(8,128)S(1)} %get-tuple-element.8.own_ref), channel_id=1, source_target_pairs={{0,16},{16,0},{32,48},{48,32},{64,80},{80,64},{96,112},{112,96},{1... | collective-permute-start | bytes 49160 | tf_op jit(solution)/shard_map/ppermute | solution.py:484
  35.1 20.6 %copy-start = (bf16[1,32,1536]{2,1,0:T(8,128)(2,1)S(1)}, bf16[1,32,1536]{2,1,0:T(8,128)(2,1)}, u32[]{:S(2)}) copy-start(bf16[1,32,1536]{2,1,0:T(8,128)(2,1)} %drift_ref.1) | copy-start | bytes 294916
  35.2 20.6 %copy-start.2 = (bf16[1,2,1536]{2,1,0:T(2,128)(2,1)S(1)}, bf16[1,2,1536]{2,1,0:T(2,128)(2,1)}, u32[]{:S(2)}) copy-start(bf16[1,2,1536]{2,1,0:T(2,128)(2,1)} %drift_norm_ref.1) | copy-start | bytes 18436
  35.2 3.5 %collective-permute-start.1 = (f32[16,40,128]{2,1,0:T(8,128)S(1)}, f32[16,40,128]{2,1,0:T(8,128)S(1)}, u32[]{:S(2)}, u32[]{:S(2)}) collective-permute-start(f32[16,40,128]{2,1,0:T(8,128)S(1)} %slice_bitcast_fusion), channel_id=1, source_target_pairs={{0,16},{16,0},{32,48},{48,32},{64,80},{80,64},{96,112},{112,96},{1... | collective-permute-start | bytes 983048 | tf_op jit(solution)/shard_map/ppermute | solution.py:490

commit v4 on v3

v4 whole, which is shorter than its diff:
```python
import functools
import operator

import jax
import jax.numpy as jnp
from jax import lax
from jax.experimental import pallas as pl
from jax.experimental.pallas import tpu as pltpu
from jax.sharding import PartitionSpec as P

K = 32
HALF = K // 2
SUB = 8
LANES = 128
SLOT = 128
UTT = 2
ROWS = UTT * SLOT
PADDED = HALF + SLOT + HALF
SHARE = 48
RUNS = 2
PARTS = 4
COT_AT = ROWS
LIVE_AT = 2 * ROWS
COUNT_AT = LIVE_AT + K
PACK_ROWS = COUNT_AT + SUB
TILE_RUN = 3

grad_factor_base = 128.0
eps_norm = 1e-05


def lane_tile(i):
    return pl.ds(pl.multiple_of(i * LANES, LANES), LANES)


def peer_rows(row, peers, tiles):
    return pl.ds(row, peers, stride=2 * tiles + 1)


WINDOWS = ((0, 3), (1, 4), (3, 3))


def share_picker(m, core):
    first, count = WINDOWS[m]
    column = lax.broadcasted_iota(jnp.int32, (1, 2 * LANES), 1)
    mine = column < LANES
    at = m * LANES + jnp.where(mine, column, column - LANES)
    shares = added([jnp.where(at >= n * SHARE, 1, 0) for n in range(1, TILE_RUN * LANES // SHARE)])
    source = at + SHARE * (shares + jnp.where(mine, core, 1 - core)) - first * LANES
    row = lax.broadcasted_iota(jnp.int32, (count * LANES, 2 * LANES), 0)
    return jnp.where(row == source, 1.0, 0.0).astype(jnp.bfloat16)


def picked(block, picker):
    return jnp.dot(block, picker, preferred_element_type=jnp.float32)


def live_rows(count):
    return lax.broadcasted_iota(jnp.int32, (SLOT, LANES), 0) < count


def added(terms):
    return functools.reduce(operator.add, terms)


def fold_rows(field):
    return jnp.sum(field.reshape(field.shape[0] // SUB, SUB, LANES), axis=0)


def scan_rows(field, upward):
    row = lax.broadcasted_iota(jnp.int32, field.shape, 0)
    step = 1
    while step < HALF:
        if upward:
            moved = jnp.where(row < HALF - step, pltpu.roll(field, HALF - step, 0), 0.0)
        else:
            moved = jnp.where(row >= step, pltpu.roll(field, step, 0), 0.0)
        field = field + moved
        step *= 2
    return field


PLAIN, NEXT, SECOND, BOTH = range(4)
PRODUCTS = (
    (PLAIN, 3),
    (SECOND, 1),
    (SECOND, 3),
    (NEXT, 2),
    (BOTH, 0),
    (BOTH, 2),
    (NEXT, 3),
    (BOTH, 1),
    (BOTH, 3),
)
COMBOS = ((0, 1, 2, 3), (0, 1), (2, 3), (0, 2), (0,), (2,), (1, 3), (1,), (3,))


def combine(parts):
    low = parts[0] + parts[1]
    high = parts[0] - parts[2]
    return (
        low + (parts[3] + parts[4]),
        low - (parts[6] + parts[7]),
        high + (parts[3] - parts[5]),
        high - (parts[6] - parts[8]),
    )


def fields_at(field_ref, i, row, product):
    kind, block = product
    return [
        field_ref[i, kind, pl.ds(row + SUB * (4 * m + block), SUB), :] for m in range(SLOT // SUB // 4)
    ]


def gate_kernel(
    count_hbm,
    glu_hbm,
    kernel_hbm,
    param_hbm,
    cot_hbm,
    own_ref,
    other_ref,
    taps_ref,
    par_ref,
    count_ref,
    glu_ref,
    kernel_ref,
    param_ref,
    cot_ref,
    small_sems,
    run_sems,
):
    channels = cot_ref.shape[1]
    width = channels // RUNS
    core = lax.rem(lax.axis_index("dp"), 2)
    small = [
        pltpu.make_async_copy(far, close, small_sems.at[n])
        for n, (far, close) in enumerate(
            ((count_hbm, count_ref), (kernel_hbm, kernel_ref), (param_hbm, param_ref))
        )
    ]
    copies = []
    for g in range(RUNS):
        for n, (far, close, at) in enumerate(
            (
                (glu_hbm, glu_ref, g * width),
                (glu_hbm, glu_ref, channels + g * width),
                (cot_hbm, cot_ref, g * width),
            )
        ):
            columns = pl.ds(at, width)
            copies.append(
                pltpu.make_async_copy(far.at[:, columns], close.at[:, columns], run_sems.at[g, n])
            )
    for copy in small + copies:
        copy.start()
    pickers = [share_picker(m, core) for m in range(TILE_RUN)]
    for copy in small:
        copy.wait()
    counts = [count_ref[u] for u in range(UTT)]
    lives = [jnp.where(live_rows(count), 1.0, 0.0) for count in counts]
    row = lax.broadcasted_iota(jnp.int32, (SUB, LANES), 0)
    count_rows = jnp.where(row == 0, counts[0], counts[1]).astype(jnp.float32)
    for g in range(RUNS):
        for copy in copies[3 * g : 3 * g + 3]:
            copy.wait()
        for m, (first, count) in enumerate(WINDOWS):
            t = g * TILE_RUN + m
            start = g * width + first * LANES
            span = count * LANES
            both = pickers[m]
            gated = picked(glu_ref[:, start : start + span], both) * jax.nn.sigmoid(
                picked(glu_ref[:, channels + start : channels + start + span], both)
            )
            cot = picked(cot_ref[:, start : start + span], both)
            small_rows = jnp.concatenate(
                [
                    kernel_ref[0, :, start : start + span].astype(jnp.float32),
                    param_ref[0, :, start : start + span].astype(jnp.float32),
                    jnp.zeros((SUB - 2, span), jnp.float32),
                ],
                axis=0,
            ).astype(jnp.bfloat16)
            small_rows = picked(small_rows, both[:, :LANES])
            rows = [small_rows[SUB * j : SUB * (j + 1)] for j in range(K // SUB)]
            for n, combo in enumerate(COMBOS):
                taps_ref[t, n] = added([rows[j] for j in combo])
            par_ref[t] = small_rows[K:]
            for side, ref in enumerate((own_ref, other_ref)):
                lanes = slice(side * LANES, (side + 1) * LANES)
                heads = []
                tails = []
                sums = []
                for u in range(UTT):
                    part = gated[u * SLOT : (u + 1) * SLOT, lanes] * lives[u]
                    ref[t, pl.ds(u * SLOT, SLOT), :] = part
                    sums.append(fold_rows(part))
                    heads.append(part[:HALF])
                    tails.append(ref[t, pl.ds(u * SLOT + counts[u] - HALF, HALF), :])
                head = added(heads)
                ref[t, pl.ds(COT_AT, ROWS), :] = cot[:, lanes]
                ref[t, pl.ds(LIVE_AT, K), :] = jnp.sum(
                    added(sums), axis=0, keepdims=True
                ) - jnp.concatenate(
                    [scan_rows(added(tails), True), scan_rows(head, False) - head], axis=0
                )
                ref[t, pl.ds(COUNT_AT, SUB), :] = count_rows


def conv_kernel(own_ref, other_ref, taps_ref, field_ref, conv_ref, live_ref, send_ref):
    tiles = conv_ref.shape[0]
    rows_each = 2 * tiles + 1
    peers = send_ref.shape[0] // rows_each
    sources = (own_ref, own_ref, other_ref, other_ref)
    counts = [sources[u][0, pl.ds(COUNT_AT + u % UTT, 1), :] for u in range(PARTS)]
    local_frames = added(counts)
    position = lax.broadcasted_iota(jnp.int32, (SLOT, LANES), 0).astype(jnp.float32)
    for u in range(PARTS):
        live_ref[pl.ds(u * SLOT, SLOT), :] = jnp.where(position < counts[u], 1.0, 0.0)
    send_ref[peer_rows(2 * tiles, peers, tiles), :] = jnp.broadcast_to(local_frames, (peers, LANES))

    def tile(i, carry):
        edge = jnp.zeros((HALF, LANES), jnp.float32)
        total = jnp.zeros((SUB, LANES), jnp.float32)
        for u in range(PARTS):
            base = u * PADDED
            field = sources[u][i, pl.ds(u % UTT * SLOT, SLOT), :]
            field = jnp.concatenate([edge, field, edge], axis=0)
            close = field[: PADDED - SUB] - field[SUB:]
            field_ref[i, PLAIN, pl.ds(base, PADDED), :] = field
            field_ref[i, NEXT, pl.ds(base, PADDED - SUB), :] = close
            field_ref[i, SECOND, pl.ds(base, PADDED - 2 * SUB), :] = (
                field[: PADDED - 2 * SUB] - field[2 * SUB :]
            )
            field_ref[i, BOTH, pl.ds(base, PADDED - 3 * SUB), :] = (
                close[: PADDED - 3 * SUB] - close[2 * SUB :]
            )
        for u in range(PARTS):
            base = u * PADDED
            sums = [None] * (4 * len(PRODUCTS))
            for first in range(SUB):
                for n, product in enumerate(PRODUCTS):
                    tap = taps_ref[i, n, pl.ds(first, 1), :]
                    for m, field in enumerate(fields_at(field_ref, i, base + first, product)):
                        term = field * tap
                        sums[4 * n + m] = term if first == 0 else sums[4 * n + m] + term
            for m in range(SLOT // SUB // 4):
                for q, out in enumerate(combine(sums[m::4])):
                    at = pl.ds(u * SLOT + SUB * (4 * m + q), SUB)
                    conv_ref[i, at, :] = out
                    total = total + out * live_ref[at, :]
        local_mean = jnp.sum(total, axis=0, keepdims=True) / local_frames
        spread = jnp.zeros((SUB, LANES), jnp.float32)
        for u in range(PARTS):
            rows = pl.ds(u * SLOT, SLOT)
            centered = (conv_ref[i, rows, :] - local_mean) * live_ref[rows, :]
            spread = spread + fold_rows(centered * centered)
        spread = jnp.sum(spread, axis=0, keepdims=True)
        send_ref[peer_rows(i, peers, tiles), :] = jnp.broadcast_to(local_mean, (peers, LANES))
        send_ref[peer_rows(i + tiles, peers, tiles), :] = jnp.broadcast_to(spread, (peers, LANES))
        return carry

    lax.fori_loop(0, tiles, tile, 0)


def store_taps(tap_ref, field_ref, i, u, source):
    blocks = [source[SUB * q : SUB * (q + 1)] for q in range(SLOT // SUB)]
    mixes = [
        [added([blocks[4 * m + q] for q in combo]) for m in range(SLOT // SUB // 4)]
        for combo in COMBOS
    ]
    for first in range(SUB):
        parts = []
        for mix, product in zip(mixes, PRODUCTS):
            fields = fields_at(field_ref, i, u * PADDED + first, product)
            parts.append(added([x * field for x, field in zip(mix, fields)]))
        for j, out in enumerate(combine(parts)):
            at = pl.ds(SUB * (first + SUB * j), SUB)
            tap_ref[at, :] = out if u == 0 else tap_ref[at, :] + out


def load_taps(tap_ref):
    return added([tap_ref[pl.ds(row, K, stride=SUB), :] for row in range(SUB)])


def lane_in(low, high):
    lane = lax.broadcasted_iota(jnp.int32, (SUB, LANES), 1)
    return (lane >= low) & (lane < high)


def pack_chunk(chunk):
    blocks = [chunk[SUB * b : SUB * (b + 1)] for b in range(6)]
    last = pltpu.roll(blocks[5], 3 * K, 1)
    moved = [pltpu.roll(blocks[4], (3 - n) * K, 1) for n in range(3)] + [last]
    packed = [jnp.where(lane_in(0, 3 * K), blocks[n], moved[n]) for n in range(4)]
    for b in range(6):
        extra = pltpu.roll(blocks[b], LANES - K + 2 * b, 1)
        last = jnp.where(lane_in(2 * K + 2 * b, 2 * K + 2 * b + 3), extra, last)
    return packed + [last]


def unpack_chunk(packed):
    parts = [packed[SUB * n : SUB * (n + 1)] for n in range(5)]
    four = pltpu.roll(parts[0], K, 1)
    four = jnp.where(lane_in(K, 2 * K), pltpu.roll(parts[1], 2 * K, 1), four)
    four = jnp.where(lane_in(2 * K, 3 * K), pltpu.roll(parts[2], 3 * K, 1), four)
    five = jnp.where(lane_in(0, K), pltpu.roll(parts[3], K, 1), pltpu.roll(parts[4], K, 1))
    sums = jnp.concatenate(parts[:4] + [four, five], axis=0)
    at = [2 * K + 2 * b for b in range(6)]
    gain_sum = jnp.concatenate([parts[4][:, n : n + 1] for n in at], axis=0)
    shift_sum = jnp.concatenate([parts[4][:, n + 1 : n + 2] for n in at], axis=0)
    return sums, gain_sum, shift_sum, parts[4][:1, at[5] + 2 : at[5] + 3]


def back_kernel(
    stat_ref,
    own_ref,
    other_ref,
    par_ref,
    field_ref,
    conv_ref,
    live_ref,
    out_ref,
    up_ref,
    norm_ref,
):
    tiles = conv_ref.shape[0]
    pairs = out_ref.shape[0]
    per_run = TILE_RUN * LANES // SHARE
    sources = (own_ref, own_ref, other_ref, other_ref)
    local_frames = added([sources[u][0, pl.ds(COUNT_AT + u % UTT, 1), :] for u in range(PARTS)])
    counts = stat_ref[peer_rows(2 * tiles, pairs, tiles), :]
    frames = jnp.sum(counts, axis=0, keepdims=True)
    row = lax.broadcasted_iota(jnp.int32, (SUB, LANES), 0)
    rest = jnp.zeros((K - SUB, LANES), jnp.float32)

    def tile(i):
        means = stat_ref[peer_rows(i, pairs, tiles), :]
        mean_row = jnp.sum(counts * means, axis=0, keepdims=True) / frames
        apart = means - mean_row
        spread = stat_ref[peer_rows(i + tiles, pairs, tiles), :] + counts * apart * apart
        inv_row = lax.rsqrt(jnp.sum(spread, axis=0, keepdims=True) / frames + eps_norm)
        gain_row = par_ref[i, pl.ds(0, 1), :]
        shift_row = par_ref[i, pl.ds(1, 1), :]
        gain_sum = jnp.zeros((SUB, LANES), jnp.float32)
        shift_sum = jnp.zeros((SUB, LANES), jnp.float32)
        for u in range(PARTS):
            rows = pl.ds(u * SLOT, SLOT)
            live = live_ref[rows, :]
            normed = (conv_ref[i, rows, :] - mean_row) * inv_row
            norm_out = gain_row * normed + shift_row
            sig = jax.nn.sigmoid(norm_out)
            slope = sig * (1.0 + norm_out * (1.0 - sig))
            upstream = sources[u][i, pl.ds(COT_AT + u % UTT * SLOT, SLOT), :] * slope * live
            normed = normed * live
            gain_sum = gain_sum + fold_rows(upstream * normed)
            shift_sum = shift_sum + fold_rows(upstream)
            store_taps(up_ref, field_ref, i, u, upstream)
            store_taps(norm_ref, field_ref, i, u, normed)
        scale = gain_row * inv_row
        extra = jnp.where(row == 0, jnp.sum(gain_sum, axis=0, keepdims=True), local_frames)
        extra = jnp.where(row == 1, jnp.sum(shift_sum, axis=0, keepdims=True), extra)
        live_sum = own_ref[i, pl.ds(LIVE_AT, K), :] + other_ref[i, pl.ds(LIVE_AT, K), :]
        block = jnp.concatenate(
            [load_taps(up_ref) * scale, live_sum * scale, load_taps(norm_ref) * scale, extra, rest],
            axis=0,
        )
        return block.T

    def run(step, carry):
        turned = jnp.concatenate([tile(step * TILE_RUN + n) for n in range(TILE_RUN)], axis=0)
        for j in range(per_run):
            for n, part in enumerate(pack_chunk(turned[j * SHARE : (j + 1) * SHARE])):
                out_ref[step * per_run + j, pl.ds(n * SUB, SUB), :] = part
        return carry

    lax.fori_loop(0, tiles // TILE_RUN, run, 0)


def delta_kernel(sum_ref, drift_ref, drift_norm_ref, out_ref):
    share = SHARE
    channels = drift_ref.shape[2]
    total, gain_sum, shift_sum, frames = unpack_chunk(
        added([sum_ref[p] for p in range(sum_ref.shape[0])])
    )
    live_part = pltpu.roll(total, LANES - K, 1)
    norm_part = pltpu.roll(total, LANES - 2 * K, 1)
    kernel_sum = total - (shift_sum * live_part + gain_sum * norm_part) / frames
    start = lax.axis_index("dp") * share
    first = jnp.minimum(start // LANES, channels // LANES - 2)
    window = pl.ds(pl.multiple_of(first * LANES, LANES), 2 * LANES)
    drift = jnp.concatenate(
        [
            drift_ref[0, :, window].astype(jnp.float32),
            drift_norm_ref[0, :, window].astype(jnp.float32),
            jnp.zeros((LANES - K - 2, 2 * LANES), jnp.float32),
        ],
        axis=0,
    )
    drift = pltpu.roll(drift, lax.rem(2 * LANES - (start - first * LANES), 2 * LANES), 1)
    drift = drift[:, :LANES].T[:share]
    lane = lax.broadcasted_iota(jnp.int32, (share, LANES), 1)
    sums = jnp.where(lane < K, kernel_sum, jnp.where(lane == K, gain_sum, shift_sum))
    delta = (drift + (grad_factor_base / frames) * sums).astype(jnp.bfloat16).astype(jnp.float32)
    weighted = delta * frames
    block = share // 3
    lane = lane[:block]
    packed = jnp.broadcast_to(frames, (block, LANES))
    for b in range(3):
        piece = weighted[b * block : (b + 1) * block]
        moved = pltpu.roll(piece, b * K, 1) if b else piece
        packed = jnp.where((lane >= b * K) & (lane < (b + 1) * K), moved, packed)
        at = 3 * K + 2 * b
        moved = pltpu.roll(piece, at - K, 1)
        packed = jnp.where((lane >= at) & (lane < at + 2), moved, packed)
    for peer in range(out_ref.shape[0]):
        out_ref[peer] = packed


def average_kernel(sum_ref, kernel_ref, norm_ref):
    total = added([sum_ref[p] for p in range(sum_ref.shape[0])])
    block = total.shape[0]
    average = total / total[:, 3 * K + 6 : 3 * K + 7]
    average = jnp.concatenate([average, jnp.zeros((LANES - block, LANES), jnp.float32)], axis=0)
    turned = average.T
    for b in range(3):
        kernel_ref[:, b * block : (b + 1) * block] = turned[b * K : (b + 1) * K, :block]
        norm_ref[:, b * block : (b + 1) * block] = turned[3 * K + 2 * b : 3 * K + 2 * b + 2, :block]


VMEM_SPEC = pl.BlockSpec(memory_space=pltpu.VMEM)
HBM_SPEC = pl.BlockSpec(memory_space=pltpu.HBM)
PARAMS = pltpu.CompilerParams(vmem_limit_bytes=32 * 1024 * 1024)


def cost(flops):
    return pl.CostEstimate(flops=flops, bytes_accessed=0, transcendentals=0)


def gate_stage(frame_count, glu_in, kernel, norm_params, cotangent):
    tiles = cotangent.shape[1] // LANES // 2
    far = [
        pltpu.with_memory_space_constraint(x, pltpu.HBM)
        for x in (frame_count, glu_in, kernel, norm_params, cotangent)
    ]
    return pl.pallas_call(
        gate_kernel,
        out_shape=(
            jax.ShapeDtypeStruct((tiles, PACK_ROWS, LANES), jnp.float32),
            jax.ShapeDtypeStruct((tiles, PACK_ROWS, LANES), jnp.float32),
            jax.ShapeDtypeStruct((tiles, len(PRODUCTS), SUB, LANES), jnp.float32),
            jax.ShapeDtypeStruct((tiles, SUB, LANES), jnp.float32),
        ),
        in_specs=[HBM_SPEC] * 5,
        out_specs=(VMEM_SPEC,) * 4,
        scratch_shapes=[
            pltpu.SMEM((UTT,), jnp.int32),
            pltpu.VMEM(glu_in.shape, glu_in.dtype),
            pltpu.VMEM(kernel.shape, kernel.dtype),
            pltpu.VMEM(norm_params.shape, norm_params.dtype),
            pltpu.VMEM(cotangent.shape, cotangent.dtype),
            pltpu.SemaphoreType.DMA((3,)),
            pltpu.SemaphoreType.DMA((RUNS, 3)),
        ],
        compiler_params=PARAMS,
        name="gate_shares",
    )(*far)


def conv_stage(own, other, taps, peers):
    tiles = own.shape[0]
    return pl.pallas_call(
        conv_kernel,
        out_shape=(
            jax.ShapeDtypeStruct((tiles, 4, PARTS * PADDED, LANES), jnp.float32),
            jax.ShapeDtypeStruct((tiles, PARTS * SLOT, LANES), jnp.float32),
            jax.ShapeDtypeStruct((PARTS * SLOT, LANES), jnp.float32),
            jax.ShapeDtypeStruct((peers * (2 * tiles + 1), LANES), jnp.float32),
        ),
        in_specs=[VMEM_SPEC] * 3,
        out_specs=(VMEM_SPEC,) * 4,
        compiler_params=PARAMS,
        name="conv_stats",
    )(own, other, taps)


def back_stage(gathered, own, other, norm_rows, fields, conv_out, live, peers):
    return pl.pallas_call(
        back_kernel,
        out_shape=jax.ShapeDtypeStruct((peers, 5 * SUB, LANES), jnp.float32),
        in_specs=[VMEM_SPEC] * 7,
        out_specs=VMEM_SPEC,
        scratch_shapes=[
            pltpu.VMEM((K * SUB, LANES), jnp.float32),
            pltpu.VMEM((K * SUB, LANES), jnp.float32),
        ],
        compiler_params=PARAMS,
        name="tap_sums",
    )(gathered, own, other, norm_rows, fields, conv_out, live)


def on_device(glu_in, cotangent, frame_count, kernel, norm_params, drift_kernel, drift_norm):
    n_dp = lax.axis_size("dp")
    n_group = lax.axis_size("group")
    pairs = n_dp // 2
    swap = [(i, i ^ 1) for i in range(n_dp)]
    same_core = [[2 * p + core for p in range(pairs)] for core in range(2)]

    own, other, taps, norm_rows = gate_stage(frame_count, glu_in, kernel, norm_params, cotangent)
    other = lax.ppermute(other, "dp", swap)
    fields, conv_out, live, stats = conv_stage(own, other, taps, pairs)
    gathered = lax.all_to_all(
        stats.reshape(pairs, 1, -1), "dp", 0, 0, axis_index_groups=same_core
    ).reshape(stats.shape)

    tap_sums = back_stage(gathered, own, other, norm_rows, fields, conv_out, live, pairs)
    tap_sums = lax.all_to_all(tap_sums, "dp", 0, 0, axis_index_groups=same_core)

    weighted = pl.pallas_call(
        delta_kernel,
        out_shape=jax.ShapeDtypeStruct((n_group, SHARE // 3, LANES), jnp.float32),
        in_specs=[VMEM_SPEC] * 3,
        out_specs=VMEM_SPEC,
        compiler_params=PARAMS,
        name="group_delta",
    )(tap_sums, drift_kernel, drift_norm)
    weighted = lax.all_to_all(weighted, "group", 0, 0)

    return pl.pallas_call(
        average_kernel,
        out_shape=(
            jax.ShapeDtypeStruct((K, SHARE), jnp.float32),
            jax.ShapeDtypeStruct((2, SHARE), jnp.float32),
        ),
        in_specs=[VMEM_SPEC],
        out_specs=(VMEM_SPEC, VMEM_SPEC),
        compiler_params=PARAMS,
        name="group_average",
    )(weighted)


def solution(mesh):
    placed = (
        P(("dp", "group"), None),
        P(("dp", "group"), None),
        P(("dp", "group")),
        P("group", None, None),
        P("group", None, None),
        P("group", None, None),
        P("group", None, None),
    )
    return jax.shard_map(
        on_device,
        mesh=mesh,
        in_specs=placed,
        out_specs=(P(None, "dp"), P(None, "dp")),
        check_vma=False,
    )
```

time: 78.3 us -> 75 us (0.958)
  blocking collectives: 58.2 us -> 54.5 us
  starting transfers between devices: 3.84 us -> 1.92 us
  Pallas kernels: 12.5 us -> 14 us
  waiting for transfers between devices: 2.74 us -> 3.55 us
    all_to_all x2, blocking collectives: 37.1 us -> 33.5 us  [the longest x1 18.2 us: on_device(): lax.all_to_all(stats.reshape(pairs, 1, -1), 'dp', 0, 0, axis_index_groups...]
    ppermute x2 -> x1, starting transfers between devices: 3.84 us -> 1.92 us  [on_device(): other = lax.ppermute(other, 'dp', swap)]
    pallas_call x5, Pallas kernels: 12.5 us -> 14 us  [the longest x1 6.32 us: back_stage(): pl.pallas_call(back_kernel, out_shape=jax.ShapeDtypeStruct((peers, 5 * SU...]
    ppermute x2 -> x1, waiting for transfers between devices: 2.74 us -> 3.55 us  [on_device(): other = lax.ppermute(other, 'dp', swap)]
  transfers between devices with their start and end apart: 2 -> 1, of which waited for: 2 -> 1; matrix products, arithmetic and copies ran while one was open for 0% -> 0% of each run, Pallas kernels for 0% -> 0%
where the time goes in v4:
time: 75 us; the launch traced here: 74.7 us
  blocking collectives  54.5 us (73%)
  Pallas kernels  14 us (19%)
  waiting for transfers between devices  3.55 us (5%)
  starting transfers between devices  1.92 us (3%)
    all_to_all x1, blocking collectives, on_device(): weighted = lax.all_to_all(weighted, 'group', 0, 0)  21 us
    all_to_all x1, blocking collectives, on_device(): lax.all_to_all(stats.reshape(pairs, 1, -1), 'dp', 0, 0, axis_index_groups...  18.2 us
    all_to_all x1, blocking collectives, on_device(): tap_sums = lax.all_to_all(tap_sums, 'dp', 0, 0, axis_index_groups=same_core)  15.3 us
    pallas_call x1, Pallas kernels, back_stage(): pl.pallas_call(back_kernel, out_shape=jax.ShapeDtypeStruct((peers, 5 * SU...  6.32 us
    ppermute x1, waiting for transfers between devices, on_device(): other = lax.ppermute(other, 'dp', swap)  3.55 us
    pallas_call x1, Pallas kernels, gate_stage(): pl.pallas_call(gate_kernel, out_shape=(jax.ShapeDtypeStruct((tiles, PACK_...  3.32 us
    pallas_call x1, Pallas kernels, conv_stage(): pl.pallas_call(conv_kernel, out_shape=(jax.ShapeDtypeStruct((tiles, 4, PA...  3.26 us
    ppermute x1, starting transfers between devices, on_device(): other = lax.ppermute(other, 'dp', swap)  1.92 us
  transfers between devices with their start and end apart: 1, of which 1 were waited for; matrix products, arithmetic and copies ran while one was open for 0% of the time, Pallas kernels for 0%

profile of v4, /device:TPU:2, one launch (start us, length us, event | category | flops | bytes accessed | tf_op | source)
XLA Modules:
  0.0 74.7 jit_solution(12129099880824039859)
XLA Ops:
  0.6 3.3 %gate_shares.1 = (f32[6,552,128]{2,1,0:T(8,128)S(1)}, f32[6,552,128]{2,1,0:T(8,128)S(1)}, f32[6,9,8,128]{3,2,1,0:T(8,128)S(1)}, f32[6,8,128]{2,1,0:T(8,128)S(1)}) custom-call(s32[2]{0:T(128)} %count_hbm.1, bf16[256,3072]{1,0:T(8,128)(2,1)} %glu_hbm.1, bf16[1,32,1536]{2,1,0:T(8,128)(2,1)} %kernel_hbm.1, bf16[1,2,1536]{2,1,0:T(2,128)(2,1)} %param_hbm.1, ...), custom_call_target="tpu_custom_call" | custom-call | tf_op jit(solution)/shard_map/gate_shares/pallas_call | solution.py:447
  4.0 1.9 %collective-permute-start = (f32[6,552,128]{2,1,0:T(8,128)S(1)}, f32[6,552,128]{2,1,0:T(8,128)S(1)}, u32[]{:S(2)}, u32[]{:S(2)}) collective-permute-start(f32[6,552,128]{2,1,0:T(8,128)S(1)} %get-tuple-element.11), channel_id=1, source_target_pairs={{0,16},{16,0},{32,48},{48,32},{64,80},{80,64},{96,112},{112,96},{1... | collective-permute-start | bytes 5087240 | tf_op jit(solution)/shard_map/ppermute | solution.py:511
  5.9 3.6 %collective-permute-done.other_ref = f32[6,552,128]{2,1,0:T(8,128)S(1)} collective-permute-done((f32[6,552,128]{2,1,0:T(8,128)S(1)}, f32[6,552,128]{2,1,0:T(8,128)S(1)}, u32[]{:S(2)}, u32[]{:S(2)}) %collective-permute-start) | collective-permute-done | bytes 1695776 | tf_op jit(solution)/shard_map/ppermute | solution.py:511
  9.4 3.3 %conv_stats.1 = (f32[6,4,640,128]{3,2,1,0:T(8,128)S(1)}, f32[6,512,128]{2,1,0:T(8,128)S(1)}, f32[512,128]{1,0:T(8,128)S(1)}, f32[208,128]{1,0:T(8,128)S(1)}) custom-call(f32[6,552,128]{2,1,0:T(8,128)S(1)} %get-tuple-element.10.own_ref, f32[6,552,128]{2,1,0:T(8,128)S(1)} %collective-permute-done.other_ref, f32[6,9,8,128]{3,2,1,0:T(8,128)S(1)} %get-tuple-element.12.taps_ref), custom_call_target="tpu_custom_call" | custom-call | tf_op jit(solution)/shard_map/conv_stats/pallas_call | solution.py:473
  12.7 18.2 %all_to_all.15 = f32[16,1,1664]{2,1,0:T(1,128)S(1)} all-to-all(f32[16,1,1664]{2,1,0:T(1,128)S(1)} %bitcast.3), channel_id=1, replica_groups={{0,32,64,96,128,160,192,224,256,288,320,352,384,416,448,480},{16,48,80,..., dimensions={0} | all-to-all | bytes 212992 | tf_op jit(solution)/shard_map/all_to_all | solution.py:513
  30.9 0.0 copy-start
  30.9 0.0 copy-start.1
  30.9 6.3 %tap_sums.1 = f32[16,40,128]{2,1,0:T(8,128)S(1)} custom-call(f32[208,128]{1,0:T(8,128)S(1)} %bitcast.2, f32[6,552,128]{2,1,0:T(8,128)S(1)} %get-tuple-element.10.own_ref, f32[6,552,128]{2,1,0:T(8,128)S(1)} %collective-permute-done.other_ref, f32[6,8,128]{2,1,0:T(8,128)S(1)} %get-tuple-element.14.par_ref, f32[6,4,640,128]{3,2,1,0:T(8,128)S(1)} %get-tuple-element.15.field_ref, ...), custom_call_target="tpu_custom_call" | custom-call | tf_op jit(solution)/shard_map/tap_sums/pallas_call | solution.py:489
  37.3 15.3 %all_to_all.16.sum_ref = f32[16,40,128]{2,1,0:T(8,128)S(1)} all-to-all(f32[16,40,128]{2,1,0:T(8,128)S(1)} %tap_sums.1), channel_id=1, replica_groups={{0,32,64,96,128,160,192,224,256,288,320,352,384,416,448,480},{16,48,80,..., dimensions={0} | all-to-all | bytes 655360 | tf_op jit(solution)/shard_map/all_to_all | solution.py:518
  52.5 0.0 copy-done
  52.5 0.0 copy-done.1
  52.5 0.3 group_delta.1
  52.9 21.0 %all_to_all.17.sum_ref = f32[16,16,128]{2,1,0:T(8,128)S(1)} all-to-all(f32[16,16,128]{2,1,0:T(8,128)S(1)} %group_delta.1), channel_id=1, replica_groups=mesh['dp'=32,'group'=16] {'group'}, dimensions={0} | all-to-all | bytes 262144 | tf_op jit(solution)/shard_map/all_to_all | solution.py:528
  73.9 0.9 %group_average.1 = (f32[32,48]{1,0:T(8,128)}, f32[2,48]{1,0:T(2,128)}) custom-call(f32[16,16,128]{2,1,0:T(8,128)S(1)} %all_to_all.17.sum_ref), custom_call_target="tpu_custom_call" | custom-call | tf_op jit(solution)/shard_map/group_average/pallas_call | solution.py:530
Async XLA Ops:
  4.0 5.5 %collective-permute-start = (f32[6,552,128]{2,1,0:T(8,128)S(1)}, f32[6,552,128]{2,1,0:T(8,128)S(1)}, u32[]{:S(2)}, u32[]{:S(2)}) collective-permute-start(f32[6,552,128]{2,1,0:T(8,128)S(1)} %get-tuple-element.11), channel_id=1, source_target_pairs={{0,16},{16,0},{32,48},{48,32},{64,80},{80,64},{96,112},{112,96},{1... | collective-permute-start | bytes 5087240 | tf_op jit(solution)/shard_map/ppermute | solution.py:511
  30.9 21.6 %copy-start = (bf16[1,32,1536]{2,1,0:T(8,128)(2,1)S(1)}, bf16[1,32,1536]{2,1,0:T(8,128)(2,1)}, u32[]{:S(2)}) copy-start(bf16[1,32,1536]{2,1,0:T(8,128)(2,1)} %drift_ref.1) | copy-start | bytes 294916
  30.9 21.6 %copy-start.1 = (bf16[1,2,1536]{2,1,0:T(2,128)(2,1)S(1)}, bf16[1,2,1536]{2,1,0:T(2,128)(2,1)}, u32[]{:S(2)}) copy-start(bf16[1,2,1536]{2,1,0:T(2,128)(2,1)} %drift_norm_ref.1) | copy-start | bytes 18436

commit v5 on v4

--- a/solution.py
+++ b/solution.py
@@ -18,7 +18,7 @@
 PADDED = HALF + SLOT + HALF
 SHARE = 48
 RUNS = 2
-PARTS = 4
+UNROLL = 1
 COT_AT = ROWS
 LIVE_AT = 2 * ROWS
 COUNT_AT = LIVE_AT + K
@@ -208,63 +208,91 @@
                 ref[t, pl.ds(COUNT_AT, SUB), :] = count_rows
 
 
-def conv_kernel(own_ref, other_ref, taps_ref, field_ref, conv_ref, live_ref, send_ref):
+def convolve(i, source_ref, taps_ref, live_ref, field_ref, conv_ref):
+    edge = jnp.zeros((HALF, LANES), jnp.float32)
+    total = jnp.zeros((SUB, LANES), jnp.float32)
+    for u in range(UTT):
+        base = u * PADDED
+        field = source_ref[i, pl.ds(u * SLOT, SLOT), :]
+        field = jnp.concatenate([edge, field, edge], axis=0)
+        close = field[: PADDED - SUB] - field[SUB:]
+        field_ref[i, PLAIN, pl.ds(base, PADDED), :] = field
+        field_ref[i, NEXT, pl.ds(base, PADDED - SUB), :] = close
+        field_ref[i, SECOND, pl.ds(base, PADDED - 2 * SUB), :] = (
+            field[: PADDED - 2 * SUB] - field[2 * SUB :]
+        )
+        field_ref[i, BOTH, pl.ds(base, PADDED - 3 * SUB), :] = (
+            close[: PADDED - 3 * SUB] - close[2 * SUB :]
+        )
+    for u in range(UTT):
+        base = u * PADDED
+        sums = [None] * (4 * len(PRODUCTS))
+        for first in range(SUB):
+            for n, product in enumerate(PRODUCTS):
+                tap = taps_ref[i, n, pl.ds(first, 1), :]
+                for m, field in enumerate(fields_at(field_ref, i, base + first, product)):
+                    term = field * tap
+                    sums[4 * n + m] = term if first == 0 else sums[4 * n + m] + term
+        for m in range(SLOT // SUB // 4):
+            for q, out in enumerate(combine(sums[m::4])):
+                at = pl.ds(u * SLOT + SUB * (4 * m + q), SUB)
+                conv_ref[i, at, :] = out
+                total = total + out * live_ref[at, :]
+    return total
+
+
+def live_masks(source_ref, live_ref):
+    position = lax.broadcasted_iota(jnp.int32, (SLOT, LANES), 0).astype(jnp.float32)
+    counts = [source_ref[0, pl.ds(COUNT_AT + u, 1), :] for u in range(UTT)]
+    for u in range(UTT):
+        live_ref[pl.ds(u * SLOT, SLOT), :] = jnp.where(position < counts[u], 1.0, 0.0)
+    return added(counts)
+
+
+def own_conv_kernel(own_ref, taps_ref, field_ref, conv_ref, live_ref, total_ref):
+    live_masks(own_ref, live_ref)
+
+    def tile(i, carry):
+        total_ref[i] = convolve(i, own_ref, taps_ref, live_ref, field_ref, conv_ref)
+        return carry
+
+    lax.fori_loop(0, conv_ref.shape[0], tile, 0, unroll=UNROLL)
+
+
+def conv_kernel(
+    own_ref,
+    other_ref,
+    taps_ref,
+    own_conv_ref,
+    own_live_ref,
+    own_total_ref,
+    field_ref,
+    conv_ref,
+    live_ref,
+    send_ref,
+):
     tiles = conv_ref.shape[0]
-    rows_each = 2 * tiles + 1
-    peers = send_ref.shape[0] // rows_each
-    sources = (own_ref, own_ref, other_ref, other_ref)
-    counts = [sources[u][0, pl.ds(COUNT_AT + u % UTT, 1), :] for u in range(PARTS)]
-    local_frames = added(counts)
-    position = lax.broadcasted_iota(jnp.int32, (SLOT, LANES), 0).astype(jnp.float32)
-    for u in range(PARTS):
-        live_ref[pl.ds(u * SLOT, SLOT), :] = jnp.where(position < counts[u], 1.0, 0.0)
+    peers = send_ref.shape[0] // (2 * tiles + 1)
+    own_counts = [own_ref[0, pl.ds(COUNT_AT + u, 1), :] for u in range(UTT)]
+    local_frames = live_masks(other_ref, live_ref) + added(own_counts)
     send_ref[peer_rows(2 * tiles, peers, tiles), :] = jnp.broadcast_to(local_frames, (peers, LANES))
 
     def tile(i, carry):
-        edge = jnp.zeros((HALF, LANES), jnp.float32)
-        total = jnp.zeros((SUB, LANES), jnp.float32)
-        for u in range(PARTS):
-            base = u * PADDED
-            field = sources[u][i, pl.ds(u % UTT * SLOT, SLOT), :]
-            field = jnp.concatenate([edge, field, edge], axis=0)
-            close = field[: PADDED - SUB] - field[SUB:]
-            field_ref[i, PLAIN, pl.ds(base, PADDED), :] = field
-            field_ref[i, NEXT, pl.ds(base, PADDED - SUB), :] = close
-            field_ref[i, SECOND, pl.ds(base, PADDED - 2 * SUB), :] = (
-                field[: PADDED - 2 * SUB] - field[2 * SUB :]
-            )
-            field_ref[i, BOTH, pl.ds(base, PADDED - 3 * SUB), :] = (
-                close[: PADDED - 3 * SUB] - close[2 * SUB :]
-            )
-        for u in range(PARTS):
-            base = u * PADDED
-            sums = [None] * (4 * len(PRODUCTS))
-            for first in range(SUB):
-                for n, product in enumerate(PRODUCTS):
-                    tap = taps_ref[i, n, pl.ds(first, 1), :]
-                    for m, field in enumerate(fields_at(field_ref, i, base + first, product)):
-                        term = field * tap
-                        sums[4 * n + m] = term if first == 0 else sums[4 * n + m] + term
-            for m in range(SLOT // SUB // 4):
-                for q, out in enumerate(combine(sums[m::4])):
-                    at = pl.ds(u * SLOT + SUB * (4 * m + q), SUB)
-                    conv_ref[i, at, :] = out
-                    total = total + out * live_ref[at, :]
+        total = own_total_ref[i] + convolve(i, other_ref, taps_ref, live_ref, field_ref, conv_ref)
         local_mean = jnp.sum(total, axis=0, keepdims=True) / local_frames
         spread = jnp.zeros((SUB, LANES), jnp.float32)
-        for u in range(PARTS):
-            rows = pl.ds(u * SLOT, SLOT)
-            centered = (conv_ref[i, rows, :] - local_mean) * live_ref[rows, :]
+        for values, live in ((own_conv_ref, own_live_ref), (conv_ref, live_ref)):
+            centered = (values[i] - local_mean) * live[...]
             spread = spread + fold_rows(centered * centered)
         spread = jnp.sum(spread, axis=0, keepdims=True)
         send_ref[peer_rows(i, peers, tiles), :] = jnp.broadcast_to(local_mean, (peers, LANES))
         send_ref[peer_rows(i + tiles, peers, tiles), :] = jnp.broadcast_to(spread, (peers, LANES))
         return carry
 
-    lax.fori_loop(0, tiles, tile, 0)
-
-
-def store_taps(tap_ref, field_ref, i, u, source):
+    lax.fori_loop(0, tiles, tile, 0, unroll=UNROLL)
+
+
+def store_taps(tap_ref, field_ref, i, u, source, first_part):
     blocks = [source[SUB * q : SUB * (q + 1)] for q in range(SLOT // SUB)]
     mixes = [
         [added([blocks[4 * m + q] for q in combo]) for m in range(SLOT // SUB // 4)]
@@ -277,7 +305,7 @@
             parts.append(added([x * field for x, field in zip(mix, fields)]))
         for j, out in enumerate(combine(parts)):
             at = pl.ds(SUB * (first + SUB * j), SUB)
-            tap_ref[at, :] = out if u == 0 else tap_ref[at, :] + out
+            tap_ref[at, :] = out if first_part else tap_ref[at, :] + out
 
 
 def load_taps(tap_ref):
@@ -318,6 +346,9 @@
     own_ref,
     other_ref,
     par_ref,
+    own_field_ref,
+    own_conv_ref,
+    own_live_ref,
     field_ref,
     conv_ref,
     live_ref,
@@ -328,8 +359,13 @@
     tiles = conv_ref.shape[0]
     pairs = out_ref.shape[0]
     per_run = TILE_RUN * LANES // SHARE
-    sources = (own_ref, own_ref, other_ref, other_ref)
-    local_frames = added([sources[u][0, pl.ds(COUNT_AT + u % UTT, 1), :] for u in range(PARTS)])
+    sides = (
+        (own_ref, own_field_ref, own_conv_ref, own_live_ref),
+        (other_ref, field_ref, conv_ref, live_ref),
+    )
+    local_frames = added(
+        [ref[0, pl.ds(COUNT_AT + u, 1), :] for ref in (own_ref, other_ref) for u in range(UTT)]
+    )
     counts = stat_ref[peer_rows(2 * tiles, pairs, tiles), :]
     frames = jnp.sum(counts, axis=0, keepdims=True)
     row = lax.broadcasted_iota(jnp.int32, (SUB, LANES), 0)
@@ -345,19 +381,21 @@
         shift_row = par_ref[i, pl.ds(1, 1), :]
         gain_sum = jnp.zeros((SUB, LANES), jnp.float32)
         shift_sum = jnp.zeros((SUB, LANES), jnp.float32)
-        for u in range(PARTS):
+        for n in range(2 * UTT):
+            source_ref, fields_ref, values_ref, mask_ref = sides[n // UTT]
+            u = n % UTT
             rows = pl.ds(u * SLOT, SLOT)
-            live = live_ref[rows, :]
-            normed = (conv_ref[i, rows, :] - mean_row) * inv_row
+            live = mask_ref[rows, :]
+            normed = (values_ref[i, rows, :] - mean_row) * inv_row
             norm_out = gain_row * normed + shift_row
             sig = jax.nn.sigmoid(norm_out)
             slope = sig * (1.0 + norm_out * (1.0 - sig))
-            upstream = sources[u][i, pl.ds(COT_AT + u % UTT * SLOT, SLOT), :] * slope * live
+            upstream = source_ref[i, pl.ds(COT_AT + u * SLOT, SLOT), :] * slope * live
             normed = normed * live
             gain_sum = gain_sum + fold_rows(upstream * normed)
             shift_sum = shift_sum + fold_rows(upstream)
-            store_taps(up_ref, field_ref, i, u, upstream)
-            store_taps(norm_ref, field_ref, i, u, normed)
+            store_taps(up_ref, fields_ref, i, u, upstream, n == 0)
+            store_taps(norm_ref, fields_ref, i, u, normed, n == 0)
         scale = gain_row * inv_row
         extra = jnp.where(row == 0, jnp.sum(gain_sum, axis=0, keepdims=True), local_frames)
         extra = jnp.where(row == 1, jnp.sum(shift_sum, axis=0, keepdims=True), extra)
@@ -468,28 +506,46 @@
     )(*far)
 
 
-def conv_stage(own, other, taps, peers):
+def conv_outputs(tiles):
+    return (
+        jax.ShapeDtypeStruct((tiles, 4, UTT * PADDED, LANES), jnp.float32),
+        jax.ShapeDtypeStruct((tiles, ROWS, LANES), jnp.float32),
+        jax.ShapeDtypeStruct((ROWS, LANES), jnp.float32),
+    )
+
+
+def own_conv_stage(own, taps):
+    tiles = own.shape[0]
+    return pl.pallas_call(
+        own_conv_kernel,
+        out_shape=(*conv_outputs(tiles), jax.ShapeDtypeStruct((tiles, SUB, LANES), jnp.float32)),
+        in_specs=[VMEM_SPEC] * 2,
+        out_specs=(VMEM_SPEC,) * 4,
+        compiler_params=PARAMS,
+        name="own_conv",
+    )(own, taps)
+
+
+def conv_stage(own, other, taps, own_conv, own_live, own_total, peers):
     tiles = own.shape[0]
     return pl.pallas_call(
         conv_kernel,
         out_shape=(
-            jax.ShapeDtypeStruct((tiles, 4, PARTS * PADDED, LANES), jnp.float32),
-            jax.ShapeDtypeStruct((tiles, PARTS * SLOT, LANES), jnp.float32),
-            jax.ShapeDtypeStruct((PARTS * SLOT, LANES), jnp.float32),
+            *conv_outputs(tiles),
             jax.ShapeDtypeStruct((peers * (2 * tiles + 1), LANES), jnp.float32),
         ),
-        in_specs=[VMEM_SPEC] * 3,
+        in_specs=[VMEM_SPEC] * 6,
         out_specs=(VMEM_SPEC,) * 4,
         compiler_params=PARAMS,
         name="conv_stats",
-    )(own, other, taps)
-
-
-def back_stage(gathered, own, other, norm_rows, fields, conv_out, live, peers):
+    )(own, other, taps, own_conv, own_live, own_total)
+
+
+def back_stage(gathered, own, other, norm_rows, own_side, other_side, peers):
     return pl.pallas_call(
         back_kernel,
         out_shape=jax.ShapeDtypeStruct((peers, 5 * SUB, LANES), jnp.float32),
-        in_specs=[VMEM_SPEC] * 7,
+        in_specs=[VMEM_SPEC] * 10,
         out_specs=VMEM_SPEC,
         scratch_shapes=[
             pltpu.VMEM((K * SUB, LANES), jnp.float32),
@@ -497,7 +553,7 @@
         ],
         compiler_params=PARAMS,
         name="tap_sums",
-    )(gathered, own, other, norm_rows, fields, conv_out, live)
+    )(gathered, own, other, norm_rows, *own_side, *other_side)
 
 
 def on_device(glu_in, cotangent, frame_count, kernel, norm_params, drift_kernel, drift_norm):
@@ -509,12 +565,13 @@
 
     own, other, taps, norm_rows = gate_stage(frame_count, glu_in, kernel, norm_params, cotangent)
     other = lax.ppermute(other, "dp", swap)
-    fields, conv_out, live, stats = conv_stage(own, other, taps, pairs)
+    *own_side, own_total = own_conv_stage(own, taps)
+    *other_side, stats = conv_stage(own, other, taps, own_side[1], own_side[2], own_total, pairs)
     gathered = lax.all_to_all(
         stats.reshape(pairs, 1, -1), "dp", 0, 0, axis_index_groups=same_core
     ).reshape(stats.shape)
 
-    tap_sums = back_stage(gathered, own, other, norm_rows, fields, conv_out, live, pairs)
+    tap_sums = back_stage(gathered, own, other, norm_rows, own_side, other_side, pairs)
     tap_sums = lax.all_to_all(tap_sums, "dp", 0, 0, axis_index_groups=same_core)
 
     weighted = pl.pallas_call(

time: 75 us -> 74.2 us (0.989)
  waiting for transfers between devices: 3.55 us -> 2.07 us
  Pallas kernels: 14 us -> 14.8 us
    ppermute x1, waiting for transfers between devices: 3.55 us -> 2.07 us  [on_device(): other = lax.ppermute(other, 'dp', swap)]
    pallas_call x1 -> x2, Pallas kernels: 3.26 us -> 3.35 us  [the longest x1 1.87 us: conv_stage(): pl.pallas_call(conv_kernel, out_shape=(*conv_outputs(tiles), jax.ShapeDty...]
  transfers between devices with their start and end apart: 1 -> 1, of which waited for: 1 -> 1; matrix products, arithmetic and copies ran while one was open for 0% -> 0% of each run, Pallas kernels for 0% -> 2%
where the time goes in v5:
time: 74.2 us; the launch traced here: 74 us
  blocking collectives  54.5 us (73%)
  Pallas kernels  14.8 us (20%)
  waiting for transfers between devices  2.07 us (3%)
  starting transfers between devices  1.92 us (3%)
    all_to_all x1, blocking collectives, on_device(): weighted = lax.all_to_all(weighted, 'group', 0, 0)  21 us
    all_to_all x1, blocking collectives, on_device(): lax.all_to_all(stats.reshape(pairs, 1, -1), 'dp', 0, 0, axis_index_groups...  18.2 us
    all_to_all x1, blocking collectives, on_device(): tap_sums = lax.all_to_all(tap_sums, 'dp', 0, 0, axis_index_groups=same_core)  15.3 us
    pallas_call x1, Pallas kernels, back_stage(): pl.pallas_call(back_kernel, out_shape=jax.ShapeDtypeStruct((peers, 5 * SU...  6.94 us
    pallas_call x1, Pallas kernels, gate_stage(): pl.pallas_call(gate_kernel, out_shape=(jax.ShapeDtypeStruct((tiles, PACK_...  3.32 us
    ppermute x1, waiting for transfers between devices, on_device(): other = lax.ppermute(other, 'dp', swap)  2.07 us
    ppermute x1, starting transfers between devices, on_device(): other = lax.ppermute(other, 'dp', swap)  1.92 us
    pallas_call x1, Pallas kernels, conv_stage(): pl.pallas_call(conv_kernel, out_shape=(*conv_outputs(tiles), jax.ShapeDty...  1.87 us
  transfers between devices with their start and end apart: 1, of which 1 were waited for; matrix products, arithmetic and copies ran while one was open for 0% of the time, Pallas kernels for 2%

profile of v5, /device:TPU:2, one launch (start us, length us, event | category | flops | bytes accessed | tf_op | source)
XLA Modules:
  0.0 74.0 jit_solution(10950166918350452519)
XLA Ops:
  0.6 3.3 %gate_shares.1 = (f32[6,552,128]{2,1,0:T(8,128)S(1)}, f32[6,552,128]{2,1,0:T(8,128)S(1)}, f32[6,9,8,128]{3,2,1,0:T(8,128)S(1)}, f32[6,8,128]{2,1,0:T(8,128)S(1)}) custom-call(s32[2]{0:T(128)} %count_hbm.1, bf16[256,3072]{1,0:T(8,128)(2,1)} %glu_hbm.1, bf16[1,32,1536]{2,1,0:T(8,128)(2,1)} %kernel_hbm.1, bf16[1,2,1536]{2,1,0:T(2,128)(2,1)} %param_hbm.1, ...), custom_call_target="tpu_custom_call" | custom-call | tf_op jit(solution)/shard_map/gate_shares/pallas_call | solution.py:485
  4.0 1.9 %collective-permute-start = (f32[6,552,128]{2,1,0:T(8,128)S(1)}, f32[6,552,128]{2,1,0:T(8,128)S(1)}, u32[]{:S(2)}, u32[]{:S(2)}) collective-permute-start(f32[6,552,128]{2,1,0:T(8,128)S(1)} %get-tuple-element.15), channel_id=1, source_target_pairs={{0,16},{16,0},{32,48},{48,32},{64,80},{80,64},{96,112},{112,96},{1... | collective-permute-start | bytes 5087240 | tf_op jit(solution)/shard_map/ppermute | solution.py:567
  5.9 1.5 %own_conv.1 = (f32[6,4,320,128]{3,2,1,0:T(8,128)S(1)}, f32[6,256,128]{2,1,0:T(8,128)S(1)}, f32[256,128]{1,0:T(8,128)S(1)}, f32[6,8,128]{2,1,0:T(8,128)S(1)}) custom-call(f32[6,552,128]{2,1,0:T(8,128)S(1)} %get-tuple-element.14.own_ref, f32[6,9,8,128]{3,2,1,0:T(8,128)S(1)} %get-tuple-element.16.taps_ref), custom_call_target="tpu_custom_call" | custom-call | tf_op jit(solution)/shard_map/own_conv/pallas_call | solution.py:519
  7.4 2.1 %collective-permute-done.other_ref = f32[6,552,128]{2,1,0:T(8,128)S(1)} collective-permute-done((f32[6,552,128]{2,1,0:T(8,128)S(1)}, f32[6,552,128]{2,1,0:T(8,128)S(1)}, u32[]{:S(2)}, u32[]{:S(2)}) %collective-permute-start) | collective-permute-done | bytes 1695776 | tf_op jit(solution)/shard_map/ppermute | solution.py:567
  9.4 1.9 %conv_stats.1 = (f32[6,4,320,128]{3,2,1,0:T(8,128)S(1)}, f32[6,256,128]{2,1,0:T(8,128)S(1)}, f32[256,128]{1,0:T(8,128)S(1)}, f32[208,128]{1,0:T(8,128)S(1)}) custom-call(f32[6,552,128]{2,1,0:T(8,128)S(1)} %get-tuple-element.14.own_ref, f32[6,552,128]{2,1,0:T(8,128)S(1)} %collective-permute-done.other_ref, f32[6,9,8,128]{3,2,1,0:T(8,128)S(1)} %get-tuple-element.16.taps_ref, ...), custom_call_target="tpu_custom_call" | custom-call | tf_op jit(solution)/shard_map/conv_stats/pallas_call | solution.py:531
  11.3 18.2 %all_to_all.15 = f32[16,1,1664]{2,1,0:T(1,128)S(1)} all-to-all(f32[16,1,1664]{2,1,0:T(1,128)S(1)} %bitcast.3), channel_id=1, replica_groups={{0,32,64,96,128,160,192,224,256,288,320,352,384,416,448,480},{16,48,80,..., dimensions={0} | all-to-all | bytes 212992 | tf_op jit(solution)/shard_map/all_to_all | solution.py:570
  29.5 0.0 copy-start
  29.5 0.0 copy-start.1
  29.5 6.9 %tap_sums.1 = f32[16,40,128]{2,1,0:T(8,128)S(1)} custom-call(f32[208,128]{1,0:T(8,128)S(1)} %bitcast.2, f32[6,552,128]{2,1,0:T(8,128)S(1)} %get-tuple-element.14.own_ref, f32[6,552,128]{2,1,0:T(8,128)S(1)} %collective-permute-done.other_ref, f32[6,8,128]{2,1,0:T(8,128)S(1)} %get-tuple-element.21.par_ref, ...), custom_call_target="tpu_custom_call" | custom-call | tf_op jit(solution)/shard_map/tap_sums/pallas_call | solution.py:545
  36.5 15.3 %all_to_all.16.sum_ref = f32[16,40,128]{2,1,0:T(8,128)S(1)} all-to-all(f32[16,40,128]{2,1,0:T(8,128)S(1)} %tap_sums.1), channel_id=1, replica_groups={{0,32,64,96,128,160,192,224,256,288,320,352,384,416,448,480},{16,48,80,..., dimensions={0} | all-to-all | bytes 655360 | tf_op jit(solution)/shard_map/all_to_all | solution.py:575
  51.8 0.0 copy-done
  51.8 0.0 copy-done.1
  51.8 0.3 group_delta.1
  52.1 21.0 %all_to_all.17.sum_ref = f32[16,16,128]{2,1,0:T(8,128)S(1)} all-to-all(f32[16,16,128]{2,1,0:T(8,128)S(1)} %group_delta.1), channel_id=1, replica_groups=mesh['dp'=32,'group'=16] {'group'}, dimensions={0} | all-to-all | bytes 262144 | tf_op jit(solution)/shard_map/all_to_all | solution.py:585
  73.1 0.9 %group_average.1 = (f32[32,48]{1,0:T(8,128)}, f32[2,48]{1,0:T(2,128)}) custom-call(f32[16,16,128]{2,1,0:T(8,128)S(1)} %all_to_all.17.sum_ref), custom_call_target="tpu_custom_call" | custom-call | tf_op jit(solution)/shard_map/group_average/pallas_call | solution.py:587
Async XLA Ops:
  4.0 5.5 %collective-permute-start = (f32[6,552,128]{2,1,0:T(8,128)S(1)}, f32[6,552,128]{2,1,0:T(8,128)S(1)}, u32[]{:S(2)}, u32[]{:S(2)}) collective-permute-start(f32[6,552,128]{2,1,0:T(8,128)S(1)} %get-tuple-element.15), channel_id=1, source_target_pairs={{0,16},{16,0},{32,48},{48,32},{64,80},{80,64},{96,112},{112,96},{1... | collective-permute-start | bytes 5087240 | tf_op jit(solution)/shard_map/ppermute | solution.py:567
  29.5 22.2 %copy-start = (bf16[1,32,1536]{2,1,0:T(8,128)(2,1)S(1)}, bf16[1,32,1536]{2,1,0:T(8,128)(2,1)}, u32[]{:S(2)}) copy-start(bf16[1,32,1536]{2,1,0:T(8,128)(2,1)} %drift_ref.1) | copy-start | bytes 294916
  29.5 22.2 %copy-start.1 = (bf16[1,2,1536]{2,1,0:T(2,128)(2,1)S(1)}, bf16[1,2,1536]{2,1,0:T(2,128)(2,1)}, u32[]{:S(2)}) copy-start(bf16[1,2,1536]{2,1,0:T(2,128)(2,1)} %drift_norm_ref.1) | copy-start | bytes 18436

commit v6 on v5

--- a/solution.py
+++ b/solution.py
@@ -18,7 +18,7 @@
 PADDED = HALF + SLOT + HALF
 SHARE = 48
 RUNS = 2
-UNROLL = 1
+UNROLL = 2
 COT_AT = ROWS
 LIVE_AT = 2 * ROWS
 COUNT_AT = LIVE_AT + K

time: 74.2 us -> 74.1 us (level)
  no operation moved by 1% of the time
where the time goes in v6:
time: 74.1 us; the launch traced here: 73.8 us
  blocking collectives  54.5 us (74%)
  Pallas kernels  14.6 us (20%)
  waiting for transfers between devices  2.15 us (3%)
  starting transfers between devices  1.92 us (3%)
    all_to_all x1, blocking collectives, on_device(): weighted = lax.all_to_all(weighted, 'group', 0, 0)  21 us
    all_to_all x1, blocking collectives, on_device(): lax.all_to_all(stats.reshape(pairs, 1, -1), 'dp', 0, 0, axis_index_groups...  18.2 us
    all_to_all x1, blocking collectives, on_device(): tap_sums = lax.all_to_all(tap_sums, 'dp', 0, 0, axis_index_groups=same_core)  15.3 us
    pallas_call x1, Pallas kernels, back_stage(): pl.pallas_call(back_kernel, out_shape=jax.ShapeDtypeStruct((peers, 5 * SU...  6.94 us
    pallas_call x1, Pallas kernels, gate_stage(): pl.pallas_call(gate_kernel, out_shape=(jax.ShapeDtypeStruct((tiles, PACK_...  3.32 us
    ppermute x1, waiting for transfers between devices, on_device(): other = lax.ppermute(other, 'dp', swap)  2.15 us
    ppermute x1, starting transfers between devices, on_device(): other = lax.ppermute(other, 'dp', swap)  1.92 us
    pallas_call x1, Pallas kernels, conv_stage(): pl.pallas_call(conv_kernel, out_shape=(*conv_outputs(tiles), jax.ShapeDty...  1.77 us
  transfers between devices with their start and end apart: 1, of which 1 were waited for; matrix products, arithmetic and copies ran while one was open for 0% of the time, Pallas kernels for 2%

profile of v6, /device:TPU:2, one launch (start us, length us, event | category | flops | bytes accessed | tf_op | source)
XLA Modules:
  0.0 73.8 jit_solution(18445907212352909272)
XLA Ops:
  0.6 3.3 %gate_shares.1 = (f32[6,552,128]{2,1,0:T(8,128)S(1)}, f32[6,552,128]{2,1,0:T(8,128)S(1)}, f32[6,9,8,128]{3,2,1,0:T(8,128)S(1)}, f32[6,8,128]{2,1,0:T(8,128)S(1)}) custom-call(s32[2]{0:T(128)} %count_hbm.1, bf16[256,3072]{1,0:T(8,128)(2,1)} %glu_hbm.1, bf16[1,32,1536]{2,1,0:T(8,128)(2,1)} %kernel_hbm.1, bf16[1,2,1536]{2,1,0:T(2,128)(2,1)} %param_hbm.1, ...), custom_call_target="tpu_custom_call" | custom-call | tf_op jit(solution)/shard_map/gate_shares/pallas_call | solution.py:485
  4.0 1.9 %collective-permute-start = (f32[6,552,128]{2,1,0:T(8,128)S(1)}, f32[6,552,128]{2,1,0:T(8,128)S(1)}, u32[]{:S(2)}, u32[]{:S(2)}) collective-permute-start(f32[6,552,128]{2,1,0:T(8,128)S(1)} %get-tuple-element.15), channel_id=1, source_target_pairs={{0,16},{16,0},{32,48},{48,32},{64,80},{80,64},{96,112},{112,96},{1... | collective-permute-start | bytes 5087240 | tf_op jit(solution)/shard_map/ppermute | solution.py:567
  5.9 1.4 %own_conv.1 = (f32[6,4,320,128]{3,2,1,0:T(8,128)S(1)}, f32[6,256,128]{2,1,0:T(8,128)S(1)}, f32[256,128]{1,0:T(8,128)S(1)}, f32[6,8,128]{2,1,0:T(8,128)S(1)}) custom-call(f32[6,552,128]{2,1,0:T(8,128)S(1)} %get-tuple-element.14.own_ref, f32[6,9,8,128]{3,2,1,0:T(8,128)S(1)} %get-tuple-element.16.taps_ref), custom_call_target="tpu_custom_call" | custom-call | tf_op jit(solution)/shard_map/own_conv/pallas_call | solution.py:519
  7.3 2.2 %collective-permute-done.other_ref = f32[6,552,128]{2,1,0:T(8,128)S(1)} collective-permute-done((f32[6,552,128]{2,1,0:T(8,128)S(1)}, f32[6,552,128]{2,1,0:T(8,128)S(1)}, u32[]{:S(2)}, u32[]{:S(2)}) %collective-permute-start) | collective-permute-done | bytes 1695776 | tf_op jit(solution)/shard_map/ppermute | solution.py:567
  9.4 1.8 %conv_stats.1 = (f32[6,4,320,128]{3,2,1,0:T(8,128)S(1)}, f32[6,256,128]{2,1,0:T(8,128)S(1)}, f32[256,128]{1,0:T(8,128)S(1)}, f32[208,128]{1,0:T(8,128)S(1)}) custom-call(f32[6,552,128]{2,1,0:T(8,128)S(1)} %get-tuple-element.14.own_ref, f32[6,552,128]{2,1,0:T(8,128)S(1)} %collective-permute-done.other_ref, f32[6,9,8,128]{3,2,1,0:T(8,128)S(1)} %get-tuple-element.16.taps_ref, ...), custom_call_target="tpu_custom_call" | custom-call | tf_op jit(solution)/shard_map/conv_stats/pallas_call | solution.py:531
  11.2 18.2 %all_to_all.15 = f32[16,1,1664]{2,1,0:T(1,128)S(1)} all-to-all(f32[16,1,1664]{2,1,0:T(1,128)S(1)} %bitcast.3), channel_id=1, replica_groups={{0,32,64,96,128,160,192,224,256,288,320,352,384,416,448,480},{16,48,80,..., dimensions={0} | all-to-all | bytes 212992 | tf_op jit(solution)/shard_map/all_to_all | solution.py:570
  29.4 0.0 copy-start
  29.4 0.0 copy-start.1
  29.4 6.9 %tap_sums.1 = f32[16,40,128]{2,1,0:T(8,128)S(1)} custom-call(f32[208,128]{1,0:T(8,128)S(1)} %bitcast.2, f32[6,552,128]{2,1,0:T(8,128)S(1)} %get-tuple-element.14.own_ref, f32[6,552,128]{2,1,0:T(8,128)S(1)} %collective-permute-done.other_ref, f32[6,8,128]{2,1,0:T(8,128)S(1)} %get-tuple-element.21.par_ref, ...), custom_call_target="tpu_custom_call" | custom-call | tf_op jit(solution)/shard_map/tap_sums/pallas_call | solution.py:545
  36.4 15.3 %all_to_all.16.sum_ref = f32[16,40,128]{2,1,0:T(8,128)S(1)} all-to-all(f32[16,40,128]{2,1,0:T(8,128)S(1)} %tap_sums.1), channel_id=1, replica_groups={{0,32,64,96,128,160,192,224,256,288,320,352,384,416,448,480},{16,48,80,..., dimensions={0} | all-to-all | bytes 655360 | tf_op jit(solution)/shard_map/all_to_all | solution.py:575
  51.7 0.0 copy-done
  51.7 0.0 copy-done.1
  51.7 0.3 group_delta.1
  52.0 21.0 %all_to_all.17.sum_ref = f32[16,16,128]{2,1,0:T(8,128)S(1)} all-to-all(f32[16,16,128]{2,1,0:T(8,128)S(1)} %group_delta.1), channel_id=1, replica_groups=mesh['dp'=32,'group'=16] {'group'}, dimensions={0} | all-to-all | bytes 262144 | tf_op jit(solution)/shard_map/all_to_all | solution.py:585
  73.0 0.9 %group_average.1 = (f32[32,48]{1,0:T(8,128)}, f32[2,48]{1,0:T(2,128)}) custom-call(f32[16,16,128]{2,1,0:T(8,128)S(1)} %all_to_all.17.sum_ref), custom_call_target="tpu_custom_call" | custom-call | tf_op jit(solution)/shard_map/group_average/pallas_call | solution.py:587
Async XLA Ops:
  4.0 5.5 %collective-permute-start = (f32[6,552,128]{2,1,0:T(8,128)S(1)}, f32[6,552,128]{2,1,0:T(8,128)S(1)}, u32[]{:S(2)}, u32[]{:S(2)}) collective-permute-start(f32[6,552,128]{2,1,0:T(8,128)S(1)} %get-tuple-element.15), channel_id=1, source_target_pairs={{0,16},{16,0},{32,48},{48,32},{64,80},{80,64},{96,112},{112,96},{1... | collective-permute-start | bytes 5087240 | tf_op jit(solution)/shard_map/ppermute | solution.py:567
  29.4 22.2 %copy-start = (bf16[1,32,1536]{2,1,0:T(8,128)(2,1)S(1)}, bf16[1,32,1536]{2,1,0:T(8,128)(2,1)}, u32[]{:S(2)}) copy-start(bf16[1,32,1536]{2,1,0:T(8,128)(2,1)} %drift_ref.1) | copy-start | bytes 294916
  29.4 22.2 %copy-start.1 = (bf16[1,2,1536]{2,1,0:T(2,128)(2,1)S(1)}, bf16[1,2,1536]{2,1,0:T(2,128)(2,1)}, u32[]{:S(2)}) copy-start(bf16[1,2,1536]{2,1,0:T(2,128)(2,1)} %drift_norm_ref.1) | copy-start | bytes 18436

commit v7 on v6

--- a/solution.py
+++ b/solution.py
@@ -18,7 +18,7 @@
 PADDED = HALF + SLOT + HALF
 SHARE = 48
 RUNS = 2
-UNROLL = 2
+UNROLL = 3
 COT_AT = ROWS
 LIVE_AT = 2 * ROWS
 COUNT_AT = LIVE_AT + K

time: 74.1 us -> 74.2 us (level)
  no operation moved by 1% of the time
where the time goes in v7:
time: 74.2 us; the launch traced here: 73.9 us
  blocking collectives  54.5 us (73%)
  Pallas kernels  14.7 us (20%)
  waiting for transfers between devices  2.09 us (3%)
  starting transfers between devices  1.92 us (3%)
    all_to_all x1, blocking collectives, on_device(): weighted = lax.all_to_all(weighted, 'group', 0, 0)  21 us
    all_to_all x1, blocking collectives, on_device(): lax.all_to_all(stats.reshape(pairs, 1, -1), 'dp', 0, 0, axis_index_groups...  18.2 us
    all_to_all x1, blocking collectives, on_device(): tap_sums = lax.all_to_all(tap_sums, 'dp', 0, 0, axis_index_groups=same_core)  15.3 us
    pallas_call x1, Pallas kernels, back_stage(): pl.pallas_call(back_kernel, out_shape=jax.ShapeDtypeStruct((peers, 5 * SU...  6.94 us
    pallas_call x1, Pallas kernels, gate_stage(): pl.pallas_call(gate_kernel, out_shape=(jax.ShapeDtypeStruct((tiles, PACK_...  3.32 us
    ppermute x1, waiting for transfers between devices, on_device(): other = lax.ppermute(other, 'dp', swap)  2.09 us
    ppermute x1, starting transfers between devices, on_device(): other = lax.ppermute(other, 'dp', swap)  1.92 us
    pallas_call x1, Pallas kernels, conv_stage(): pl.pallas_call(conv_kernel, out_shape=(*conv_outputs(tiles), jax.ShapeDty...  1.83 us
  transfers between devices with their start and end apart: 1, of which 1 were waited for; matrix products, arithmetic and copies ran while one was open for 0% of the time, Pallas kernels for 2%

profile of v7, /device:TPU:2, one launch (start us, length us, event | category | flops | bytes accessed | tf_op | source)
XLA Modules:
  0.0 73.9 jit_solution(7752202281570706652)
XLA Ops:
  0.6 3.3 %gate_shares.1 = (f32[6,552,128]{2,1,0:T(8,128)S(1)}, f32[6,552,128]{2,1,0:T(8,128)S(1)}, f32[6,9,8,128]{3,2,1,0:T(8,128)S(1)}, f32[6,8,128]{2,1,0:T(8,128)S(1)}) custom-call(s32[2]{0:T(128)} %count_hbm.1, bf16[256,3072]{1,0:T(8,128)(2,1)} %glu_hbm.1, bf16[1,32,1536]{2,1,0:T(8,128)(2,1)} %kernel_hbm.1, bf16[1,2,1536]{2,1,0:T(2,128)(2,1)} %param_hbm.1, ...), custom_call_target="tpu_custom_call" | custom-call | tf_op jit(solution)/shard_map/gate_shares/pallas_call | solution.py:485
  4.0 1.9 %collective-permute-start = (f32[6,552,128]{2,1,0:T(8,128)S(1)}, f32[6,552,128]{2,1,0:T(8,128)S(1)}, u32[]{:S(2)}, u32[]{:S(2)}) collective-permute-start(f32[6,552,128]{2,1,0:T(8,128)S(1)} %get-tuple-element.15), channel_id=1, source_target_pairs={{0,16},{16,0},{32,48},{48,32},{64,80},{80,64},{96,112},{112,96},{1... | collective-permute-start | bytes 5087240 | tf_op jit(solution)/shard_map/ppermute | solution.py:567
  5.9 1.5 %own_conv.1 = (f32[6,4,320,128]{3,2,1,0:T(8,128)S(1)}, f32[6,256,128]{2,1,0:T(8,128)S(1)}, f32[256,128]{1,0:T(8,128)S(1)}, f32[6,8,128]{2,1,0:T(8,128)S(1)}) custom-call(f32[6,552,128]{2,1,0:T(8,128)S(1)} %get-tuple-element.14.own_ref, f32[6,9,8,128]{3,2,1,0:T(8,128)S(1)} %get-tuple-element.16.taps_ref), custom_call_target="tpu_custom_call" | custom-call | tf_op jit(solution)/shard_map/own_conv/pallas_call | solution.py:519
  7.4 2.1 %collective-permute-done.other_ref = f32[6,552,128]{2,1,0:T(8,128)S(1)} collective-permute-done((f32[6,552,128]{2,1,0:T(8,128)S(1)}, f32[6,552,128]{2,1,0:T(8,128)S(1)}, u32[]{:S(2)}, u32[]{:S(2)}) %collective-permute-start) | collective-permute-done | bytes 1695776 | tf_op jit(solution)/shard_map/ppermute | solution.py:567
  9.4 1.8 %conv_stats.1 = (f32[6,4,320,128]{3,2,1,0:T(8,128)S(1)}, f32[6,256,128]{2,1,0:T(8,128)S(1)}, f32[256,128]{1,0:T(8,128)S(1)}, f32[208,128]{1,0:T(8,128)S(1)}) custom-call(f32[6,552,128]{2,1,0:T(8,128)S(1)} %get-tuple-element.14.own_ref, f32[6,552,128]{2,1,0:T(8,128)S(1)} %collective-permute-done.other_ref, f32[6,9,8,128]{3,2,1,0:T(8,128)S(1)} %get-tuple-element.16.taps_ref, ...), custom_call_target="tpu_custom_call" | custom-call | tf_op jit(solution)/shard_map/conv_stats/pallas_call | solution.py:531
  11.3 18.2 %all_to_all.15 = f32[16,1,1664]{2,1,0:T(1,128)S(1)} all-to-all(f32[16,1,1664]{2,1,0:T(1,128)S(1)} %bitcast.3), channel_id=1, replica_groups={{0,32,64,96,128,160,192,224,256,288,320,352,384,416,448,480},{16,48,80,..., dimensions={0} | all-to-all | bytes 212992 | tf_op jit(solution)/shard_map/all_to_all | solution.py:570
  29.5 0.0 copy-start
  29.5 0.0 copy-start.1
  29.5 6.9 %tap_sums.1 = f32[16,40,128]{2,1,0:T(8,128)S(1)} custom-call(f32[208,128]{1,0:T(8,128)S(1)} %bitcast.2, f32[6,552,128]{2,1,0:T(8,128)S(1)} %get-tuple-element.14.own_ref, f32[6,552,128]{2,1,0:T(8,128)S(1)} %collective-permute-done.other_ref, f32[6,8,128]{2,1,0:T(8,128)S(1)} %get-tuple-element.21.par_ref, ...), custom_call_target="tpu_custom_call" | custom-call | tf_op jit(solution)/shard_map/tap_sums/pallas_call | solution.py:545
  36.5 15.3 %all_to_all.16.sum_ref = f32[16,40,128]{2,1,0:T(8,128)S(1)} all-to-all(f32[16,40,128]{2,1,0:T(8,128)S(1)} %tap_sums.1), channel_id=1, replica_groups={{0,32,64,96,128,160,192,224,256,288,320,352,384,416,448,480},{16,48,80,..., dimensions={0} | all-to-all | bytes 655360 | tf_op jit(solution)/shard_map/all_to_all | solution.py:575
  51.7 0.0 copy-done
  51.7 0.0 copy-done.1
  51.7 0.3 group_delta.1
  52.0 21.0 %all_to_all.17.sum_ref = f32[16,16,128]{2,1,0:T(8,128)S(1)} all-to-all(f32[16,16,128]{2,1,0:T(8,128)S(1)} %group_delta.1), channel_id=1, replica_groups=mesh['dp'=32,'group'=16] {'group'}, dimensions={0} | all-to-all | bytes 262144 | tf_op jit(solution)/shard_map/all_to_all | solution.py:585
  73.1 0.9 %group_average.1 = (f32[32,48]{1,0:T(8,128)}, f32[2,48]{1,0:T(2,128)}) custom-call(f32[16,16,128]{2,1,0:T(8,128)S(1)} %all_to_all.17.sum_ref), custom_call_target="tpu_custom_call" | custom-call | tf_op jit(solution)/shard_map/group_average/pallas_call | solution.py:587
Async XLA Ops:
  4.0 5.5 %collective-permute-start = (f32[6,552,128]{2,1,0:T(8,128)S(1)}, f32[6,552,128]{2,1,0:T(8,128)S(1)}, u32[]{:S(2)}, u32[]{:S(2)}) collective-permute-start(f32[6,552,128]{2,1,0:T(8,128)S(1)} %get-tuple-element.15), channel_id=1, source_target_pairs={{0,16},{16,0},{32,48},{48,32},{64,80},{80,64},{96,112},{112,96},{1... | collective-permute-start | bytes 5087240 | tf_op jit(solution)/shard_map/ppermute | solution.py:567
  29.5 22.2 %copy-start = (bf16[1,32,1536]{2,1,0:T(8,128)(2,1)S(1)}, bf16[1,32,1536]{2,1,0:T(8,128)(2,1)}, u32[]{:S(2)}) copy-start(bf16[1,32,1536]{2,1,0:T(8,128)(2,1)} %drift_ref.1) | copy-start | bytes 294916
  29.5 22.2 %copy-start.1 = (bf16[1,2,1536]{2,1,0:T(2,128)(2,1)S(1)}, bf16[1,2,1536]{2,1,0:T(2,128)(2,1)}, u32[]{:S(2)}) copy-start(bf16[1,2,1536]{2,1,0:T(2,128)(2,1)} %drift_norm_ref.1) | copy-start | bytes 18436
